TPU v7x, 128 devices: a whole 4x4x4 slice. The times are simulated.
128 devices in a mesh: gx: 8 (over y, x_hi), gy: 4 (over z), ta: 4 (over x_lo, core).
Axes of the slice: x: 4 (x_hi: 2, x_lo: 2; x = x_hi * 2 + x_lo), y: 4, z: 4, core: 2. Of those that a mesh axis runs over, the one named last changes fastest.
Arguments:
- field: float32 [1024, 1024, 512], P('gx', 'gy', 'ta'), may hold values from -32 to 32
- init_y: float32 [1024, 64], P('gy'), may hold values from -0.1875 to 0.1875
- init_t: float32 [512, 32], P('ta'), may hold values from -0.25 to 0.25
- sketch_x: float32 [2048, 64], replicated, may hold values from -0.125 to 0.125
- sketch_y: float32 [2048, 64], replicated, may hold values from -0.125 to 0.125
- sketch_t: float32 [4096, 32], replicated, may hold values from -0.09375 to 0.09375
Outputs:
- factor_x: float32 [1024, 64], P('gx')
- factor_y: float32 [1024, 64], P('gy')
- factor_t: float32 [512, 32], P('ta')
- core: float32 [64, 2048], replicated
All inputs are finite; a program needn't handle non-finite values.
Results may differ from a plain program's by a relative error of at most 0.00024.
Values sent between devices are 32-bit elements; how exact they have to be, the bound alone decides.
No kernel may reach another device: no remote copies, remote signals or barrier semaphores. Data moves between devices by JAX's collectives and lax.ppermute only.
A program may use at most 128 MiB of HBM per device.

v0:
```python
import math

import jax
import jax.numpy as jnp
from jax import lax
from jax.experimental import pallas as pl
from jax.experimental.pallas import tpu as pltpu
from jax.sharding import Mesh, PartitionSpec as P

HIGH = lax.Precision.HIGHEST
F32 = jnp.float32
BF16 = jnp.bfloat16
VMEM = pl.BlockSpec(memory_space=pltpu.VMEM)
HBM = pl.BlockSpec(memory_space=pltpu.HBM)
SMEM = pl.BlockSpec(memory_space=pltpu.SMEM)
MOST = 61 * 1024 * 1024
BIG = 58 * 1024 * 1024
MIDDLE = 4 * 1024 * 1024


def room(size):
    return pltpu.CompilerParams(vmem_limit_bytes=size)


def split(x):
    hi = x.astype(BF16)
    return hi, (x - hi.astype(F32)).astype(BF16)


def twice(x):
    hi, lo = split(x)
    return jnp.concatenate([jnp.concatenate([hi, hi], 1), jnp.concatenate([lo, lo], 1)], 0)


def dot(a, b, da=1, db=0, precision=None):
    return lax.dot_general(
        a, b, (((da,), (db,)), ((), ())), precision=precision, preferred_element_type=F32
    )


def tree_sum(parts):
    parts = list(parts)
    while len(parts) > 1:
        even = [parts[i] + parts[i + 1] for i in range(0, len(parts) - 1, 2)]
        parts = even + parts[len(even) * 2 :]
    return parts[0]


def cholesky_inverse(g):
    n = g.shape[0]
    nb = n // 8
    lane = lax.broadcasted_iota(jnp.int32, (8, 128), 1)
    sub = lax.broadcasted_iota(jnp.int32, (8, 128), 0)
    blocks = []
    for k in range(nb):
        eye = (lane - n == sub + 8 * k).astype(F32)
        wide = jnp.concatenate([g[8 * k : 8 * k + 8, :], jnp.zeros((8, 128 - n), F32)], 1)
        blocks.append(jnp.where(lane < n, wide, eye))
    out = []
    for kb in range(nb):
        rows = blocks[kb]
        cols = [
            jnp.broadcast_to(rows[:, 8 * kb + j : 8 * kb + j + 1], (8, 128)) for j in range(8)
        ]
        done = rows
        for p in range(8):
            inv = 1.0 / cols[p][p : p + 1, :]
            at = sub == p
            done = jnp.where(at, rows * lax.rsqrt(cols[p]), done)
            pivot = rows[p : p + 1, :] * inv
            rows = jnp.where(at, pivot, rows - cols[p] * pivot)
            for j in range(p + 1, 8):
                c = cols[j][p : p + 1, :] * inv
                cols[j] = jnp.where(at, c, cols[j] - cols[p] * c)
        out.append(done)
        for m in range(kb + 1, nb):
            b = blocks[m]
            blocks[m] = b - tree_sum(
                [b[:, 8 * kb + j : 8 * kb + j + 1] * rows[j : j + 1, :] for j in range(8)]
            )
    return jnp.concatenate(out, 0)[:, n : 2 * n]


def fold(g):
    return jnp.concatenate([g[:32], g[32:]], 1)


def unfold(g):
    return jnp.concatenate([g[:, :64], g[:, 64:]], 0)


def first_kernel(field, init_t, init_y, sketch, w, z, held, pair_w, lhs, turned, proj, sems, out_sems):
    nx, ny, nt = held.shape
    r3, r2, k = init_t.shape[0], init_y.shape[0], sketch.shape[0]
    chunks = sems.shape[0]
    rows = nx // chunks

    def copy(i):
        s = pl.ds(i * rows, rows)
        return pltpu.make_async_copy(field.at[s], held.at[s], sems.at[i])

    def copy_out(i, part):
        s = pl.ds(pl.multiple_of(i * rows + part * nx, 16), rows)
        return pltpu.make_async_copy(pair_w.at[:, s, :], w.at[:, s, :], out_sems.at[i, part])

    for i in range(chunks):
        copy(i).start()
    lhs[...] = twice(init_t[...])
    for i in range(0, r2 * r3, 128):
        turned[i : i + 128, :] = sketch[:, i : i + 128].T
    hi, lo = split(init_y[...])
    rhs = jnp.concatenate([hi, hi, lo, lo], 0)
    for c in range(r3):
        hi, lo = split(turned[pl.ds(c, r2, stride=r3), :].T)
        hi, lo = split(dot(jnp.concatenate([hi, lo, hi, lo], 1), rhs))
        proj[c, :k, :] = hi
        proj[c, k:, :] = lo

    def chunk(i, _):
        copy(i).wait()
        groups = []
        for x8 in range(0, rows, 8):
            outs = []
            for x in range(8):
                hi, lo = split(held[i * rows + x8 + x])
                o = dot(lhs[...], jnp.concatenate([hi, lo], 1), 1, 1)
                outs.append(o[:r3] + o[r3:])
            groups.append(jnp.swapaxes(jnp.stack(outs, 0), 0, 1))
        hi, lo = split(jnp.concatenate(groups, 1))
        at = pl.multiple_of(i * rows, 16)
        pair_w[:, pl.ds(at, rows), :] = hi
        pair_w[:, pl.ds(pl.multiple_of(at + nx, 16), rows), :] = lo
        copy_out(i, 0).start()
        copy_out(i, 1).start()
        return 0

    lax.fori_loop(0, chunks, chunk, 0)
    acc = dot(proj[0], pair_w[0], 1, 1)
    for c in range(1, r3):
        acc += dot(proj[c], pair_w[c], 1, 1)
    z[...] = (acc[k:, :nx] + acc[:k, nx:] + acc[k:, nx:]) + acc[:k, :nx]
    for i in range(chunks):
        copy_out(i, 0).wait()
        copy_out(i, 1).wait()


def first(field, init_t, init_y, sketch):
    nx, ny, nt = field.shape
    r3, r2, k = init_t.shape[0], init_y.shape[0], sketch.shape[0]
    return pl.pallas_call(
        first_kernel,
        in_specs=[HBM, VMEM, VMEM, VMEM],
        out_specs=[HBM, VMEM],
        out_shape=[
            jax.ShapeDtypeStruct((r3, 2 * nx, ny), BF16),
            jax.ShapeDtypeStruct((k, nx), F32),
        ],
        scratch_shapes=[
            pltpu.VMEM((nx, ny, nt), F32),
            pltpu.VMEM((r3, 2 * nx, ny), BF16),
            pltpu.VMEM((2 * r3, 2 * nt), BF16),
            pltpu.VMEM((r2 * r3, k), F32),
            pltpu.VMEM((r3, 2 * k, ny), BF16),
            pltpu.SemaphoreType.DMA((8,)),
            pltpu.SemaphoreType.DMA((8, 2)),
        ],
        compiler_params=room(BIG),
        cost_estimate=pl.CostEstimate(
            flops=8 * nx * ny * nt * r3, bytes_accessed=nx * ny * nt * 4, transcendentals=0
        ),
    )(field, init_t, init_y, sketch)


def gram_kernel(parts, z, gram):
    total = tree_sum([parts[i] for i in range(parts.shape[0])])
    z[...] = total
    g = fold(dot(total, total, 1, 1, HIGH))
    for i in range(gram.shape[0]):
        gram[i] = g


def gram_of(parts, copies):
    k, n = parts.shape[1:]
    return pl.pallas_call(
        gram_kernel,
        in_specs=[VMEM],
        out_specs=[VMEM, VMEM],
        out_shape=[
            jax.ShapeDtypeStruct((k, n), F32),
            jax.ShapeDtypeStruct((copies, k * k // 128, 128), F32),
        ],
        compiler_params=room(MIDDLE),
    )(parts)


def sketch_y_kernel(sketch, out, turned):
    k = sketch.shape[0]
    r3 = out.shape[0] // k
    r1 = sketch.shape[1] // r3
    for i in range(0, r1 * r3, 128):
        turned[i : i + 128, :] = sketch[:, i : i + 128].T
    for c in range(r3):
        hi, lo = split(turned[pl.ds(c, r1, stride=r3), :].T)
        out[c * k : (c + 1) * k, :] = jnp.concatenate([hi, lo, hi, lo], 1)


def prepared_y(sketch, r3):
    k, n = sketch.shape
    return pl.pallas_call(
        sketch_y_kernel,
        in_specs=[VMEM],
        out_specs=VMEM,
        out_shape=jax.ShapeDtypeStruct((r3 * k, 4 * n // r3), BF16),
        scratch_shapes=[pltpu.VMEM((n, k), F32)],
        compiler_params=room(MIDDLE),
        cost_estimate=pl.CostEstimate(flops=10**7, bytes_accessed=2 * 10**6, transcendentals=0),
    )(sketch)


def second_kernel(scale, core_id, grams, z, sk, w, q, factor, mine, other, pair_w, sems):
    r3 = pair_w.shape[0]
    each = r3 // sems.shape[0]

    def copy(i):
        s = pl.ds(i * each, each)
        return pltpu.make_async_copy(w.at[s], pair_w.at[s], sems.at[i])

    for i in range(r3 // each):
        copy(i).start()
    g = unfold(tree_sum([grams[i] for i in range(grams.shape[0])]))
    qv = dot(cholesky_inverse(g), z[...], 1, 0, HIGH)
    q[...] = qv
    factor[...] = qv * scale
    hi, lo = split(qv)
    v = dot(sk[...], jnp.concatenate([hi, hi, lo, lo], 0))
    half = mine.shape[0]
    k = 2 * half
    acc = None
    for c in range(r3):
        if c % each == 0:
            copy(c // each).wait()
        o = dot(twice(v[c * k : (c + 1) * k]), pair_w[c])
        acc = o if acc is None else acc + o
    zy = acc[k:] + acc[:k]
    first = core_id[0] == 0
    mine[...] = jnp.where(first, zy[:half], zy[half:])
    other[...] = jnp.where(first, zy[half:], zy[:half])


def second(core_id, grams, z, sk, pair_w, scale):
    r1, nx = z.shape
    r3, _, ny = pair_w.shape
    half = jax.ShapeDtypeStruct((sk.shape[0] // r3 // 2, ny), F32)
    return pl.pallas_call(
        lambda *a: second_kernel(scale, *a),
        in_specs=[SMEM, VMEM, VMEM, VMEM, HBM],
        out_specs=[VMEM] * 4,
        out_shape=[
            jax.ShapeDtypeStruct((r1, nx), F32),
            jax.ShapeDtypeStruct((r1, nx), F32),
            half,
            half,
        ],
        scratch_shapes=[pltpu.VMEM(pair_w.shape, BF16), pltpu.SemaphoreType.DMA((4,))],
        compiler_params=room(MOST),
    )(core_id, grams, z, sk, pair_w)


def contract_x_kernel(q, field, wx, held, out, lhs, sems, out_sems):
    nx, ny, nt = held.shape
    r1 = q.shape[0]
    chunks = sems.shape[0]
    rows = ny // chunks

    def copy(i):
        s = pl.ds(pl.multiple_of(i * rows, 8), rows)
        return pltpu.make_async_copy(field.at[:, s, :], held.at[:, s, :], sems.at[i])

    def copy_out(i):
        s = pl.ds(pl.multiple_of(i * rows, 8), rows)
        return pltpu.make_async_copy(out.at[:, s, :], wx.at[:, s, :], out_sems.at[i])

    for i in range(chunks):
        copy(i).start()
    lhs[...] = twice(q[...])

    def chunk(i, _):
        copy(i).wait()
        for y8 in range(0, rows, 8):
            at = pl.multiple_of(i * rows + y8, 8)
            f = jnp.swapaxes(held[:, pl.ds(at, 8), :], 0, 1)
            outs = []
            for y in range(0, 8, 2):
                h0, l0 = split(f[y])
                h1, l1 = split(f[y + 1])
                rhs = jnp.concatenate(
                    [jnp.concatenate([h0, h1], 1), jnp.concatenate([l0, l1], 1)], 0
                )
                o = dot(lhs[...], rhs)
                o = o[r1:] + o[:r1]
                outs += [o[:, :nt], o[:, nt:]]
            out[:, pl.ds(at, 8), :] = jnp.swapaxes(jnp.stack(outs, 0), 0, 1)
        copy_out(i).start()
        return 0

    lax.fori_loop(0, chunks, chunk, 0)
    for i in range(chunks):
        copy_out(i).wait()


def contract_x(q, field):
    nx, ny, nt = field.shape
    r1 = q.shape[0]
    return pl.pallas_call(
        contract_x_kernel,
        in_specs=[VMEM, HBM],
        out_specs=HBM,
        out_shape=jax.ShapeDtypeStruct((r1, ny, nt), F32),
        scratch_shapes=[
            pltpu.VMEM((nx, ny, nt), F32),
            pltpu.VMEM((r1, ny, nt), F32),
            pltpu.VMEM((2 * r1, 2 * nx), BF16),
            pltpu.SemaphoreType.DMA((8,)),
            pltpu.SemaphoreType.DMA((8,)),
        ],
        compiler_params=room(BIG),
        cost_estimate=pl.CostEstimate(
            flops=8 * nx * ny * nt * r1, bytes_accessed=nx * ny * nt * 6, transcendentals=0
        ),
    )(q, field)


def third_kernel(scale, grams, z, sketch, w_hbm, factor, part, zt, wx, sems):
    r1, ny, nt = wx.shape
    r2 = z.shape[0]
    chunks = sems.shape[0]
    rows = r1 // chunks

    def copy(i):
        s = pl.ds(i * rows, rows)
        return pltpu.make_async_copy(w_hbm.at[s], wx.at[s], sems.at[i])

    for i in range(chunks):
        copy(i).start()
    g = unfold(tree_sum([grams[i] for i in range(grams.shape[0])]))
    qv = dot(cholesky_inverse(g), z[...], 1, 0, HIGH)
    factor[...] = qv * scale
    hi, lo = split(qv)
    lhs = jnp.concatenate([hi, lo], 0)
    k = sketch.shape[0]
    group = rows

    def step(i, acc):
        copy(i).wait()
        for b in range(group):
            hi, lo = split(wx[i * group + b])
            o = dot(lhs, jnp.concatenate([hi, lo], 1))
            o = (o[r2:, :nt] + o[:r2, nt:] + o[r2:, nt:]) + o[:r2, :nt]
            hi, lo = split(o)
            at = pl.multiple_of(i * group * r2 + b * r2, r2)
            part[pl.ds(at, r2), :] = jnp.concatenate([hi, lo], 1)
        s = pl.ds(pl.multiple_of(i * group * r2, group * r2), group * r2)
        hi, lo = split(sketch[:, s])
        return acc + dot(jnp.concatenate([hi, lo], 0), part[s, :])

    acc = lax.fori_loop(0, r1 // group, step, jnp.zeros((2 * k, 2 * nt), F32))
    total = (acc[k:, :nt] + acc[:k, nt:] + acc[k:, nt:]) + acc[:k, :nt]
    for i in range(zt.shape[0]):
        zt[i] = total


def third(grams, z, sketch, wx, scale, copies):
    r2, ny = z.shape
    r1, _, nt = wx.shape
    k = sketch.shape[0]
    return pl.pallas_call(
        lambda *a: third_kernel(scale, *a),
        in_specs=[VMEM, VMEM, VMEM, HBM],
        out_specs=[VMEM] * 3,
        out_shape=[
            jax.ShapeDtypeStruct((r2, ny), F32),
            jax.ShapeDtypeStruct((r1 * r2, 2 * nt), BF16),
            jax.ShapeDtypeStruct((copies, k, nt), F32),
        ],
        scratch_shapes=[pltpu.VMEM(wx.shape, F32), pltpu.SemaphoreType.DMA((16,))],
        compiler_params=room(BIG),
    )(grams, z, sketch, wx)


def core_kernel(core_id, parts, part, z, gram, mine, other):
    total = tree_sum([parts[i] for i in range(parts.shape[0])])
    z[...] = total
    gram[...] = dot(total, total, 1, 1, HIGH)
    k = total.shape[0]
    lhs = twice(total)
    group = lax.broadcasted_iota(jnp.int32, (8, 128), 1) // 32
    first = core_id[0] == 0
    for i in range(part.shape[0] // 256):
        o = dot(lhs, part[i * 256 : (i + 1) * 256, :], 1, 1)
        o = o[k:] + o[:k]
        for j in range(2):
            v = [o[8 * g : 8 * g + 8, 128 * j : 128 * j + 128] for g in range(4)]
            slots = []
            for s in range(4):
                t = None
                for g in range(4):
                    shift = (g - s) * 32 % 128
                    u = pltpu.roll(v[g], shift, 1) if shift else v[g]
                    t = u if t is None else jnp.where(group == g, u, t)
                slots.append(t)
            for b in range(2):
                at = i * 4 + j * 2 + b
                mine[at] = jnp.where(first, slots[2 * b], slots[2 * b + 1])
                other[at] = jnp.where(first, slots[2 * b + 1], slots[2 * b])


def core_terms(core_id, parts, part, r1):
    k, nt = parts.shape[1:]
    slots = jax.ShapeDtypeStruct((r1, 8, 128), F32)
    return pl.pallas_call(
        core_kernel,
        in_specs=[SMEM, VMEM, VMEM],
        out_specs=[VMEM] * 4,
        out_shape=[
            jax.ShapeDtypeStruct((k, nt), F32),
            jax.ShapeDtypeStruct((k, k), F32),
            slots,
            slots,
        ],
        compiler_params=room(MIDDLE),
    )(core_id, parts, part)


def scale_kernel(scale, gram0, gram1, z, pieces, factor, out, held):
    inv = cholesky_inverse(gram0[...] + gram1[...])
    factor[...] = dot(inv, z[...], 1, 0, HIGH) * scale
    piece = tree_sum([pieces[i] for i in range(pieces.shape[0])])
    x = jnp.concatenate([piece[:, 32 * g : 32 * g + 32] for g in range(4)], 0)
    held[...] = dot(x, inv, 0, 1, HIGH)
    row = jnp.concatenate([held[pl.ds(s, 8, stride=4), :] for s in range(4)], 1)
    for i in range(out.shape[0]):
        out[i] = row


def scaled(gram0, gram1, z, pieces, scale):
    k, nt = z.shape
    return pl.pallas_call(
        lambda *a: scale_kernel(scale, *a),
        in_specs=[VMEM] * 4,
        out_specs=[VMEM] * 2,
        out_shape=[
            jax.ShapeDtypeStruct((k, nt), F32),
            jax.ShapeDtypeStruct(pieces.shape, F32),
        ],
        scratch_shapes=[pltpu.VMEM((k, k), F32)],
        compiler_params=room(MIDDLE),
    )(gram0, gram1, z, pieces)


def join_kernel(core_id, own, other, out):
    first = core_id[0] == 0
    half = out.shape[1] // 2
    for r in range(own.shape[1]):
        a = own[:, r, :]
        b = other[:, r, :]
        out[:, r * 128 : (r + 1) * 128] = jnp.where(first, a, b)
        out[:, half + r * 128 : half + (r + 1) * 128] = jnp.where(first, b, a)


def joined(core_id, own, other):
    n = own.shape[0]
    return pl.pallas_call(
        join_kernel,
        in_specs=[SMEM, VMEM, VMEM],
        out_specs=VMEM,
        out_shape=jax.ShapeDtypeStruct((n, 2 * 8 * 128), F32),
        compiler_params=room(MIDDLE),
    )(core_id, own, other)


def pair(x):
    return lax.ppermute(x, "c", [(0, 1), (1, 0)])


def exchange(x, axes):
    return lax.all_to_all(x, axes, 0, 0)


def spread(x, axes):
    n = math.prod(lax.axis_size(a) for a in axes)
    return exchange(jnp.broadcast_to(x, (n,) + x.shape), axes)


def both(x, axis):
    other = pair(x)
    first = lax.axis_index("c") == 0
    return jnp.where(
        first, jnp.concatenate([x, other], axis), jnp.concatenate([other, x], axis)
    )


def on_device(field, init_y, init_t, sketch_x, sketch_y, sketch_t):
    rows_x, rows_y, rows_t = field.shape
    r3 = init_t.shape[1]
    r1 = sketch_x.shape[1]
    scale_x = math.sqrt(rows_x * lax.axis_size(("y", "h")))
    scale_y = math.sqrt(rows_y * lax.axis_size("z"))
    scale_t = math.sqrt(rows_t * lax.axis_size(("l", "c")))
    core_id = lax.axis_index("c").astype(jnp.int32).reshape(1)

    pair_w, zx = first(field, init_t.T, init_y.T, sketch_x.T)
    zx, gx = gram_of(spread(zx + pair(zx), ("z", "l")), 8)
    sk_y = prepared_y(sketch_y.T, r3)
    qx, factor_x, mine, other = second(
        core_id, exchange(gx, ("y", "h")), zx, sk_y, pair_w, scale_x
    )
    wx = contract_x(qx, field)
    zy = spread(mine + pair(other), ("y", "h", "l")).sum(0)
    zy, wx = lax.optimization_barrier((zy, wx))
    zy = both(zy, 0)
    zy, gy = gram_of(zy[None], 4)
    factor_y, part, zt = third(exchange(gy, ("z",)), zy, sketch_t.T, wx, scale_y, 32)
    zt, gt, mine, other = core_terms(core_id, exchange(zt, ("y", "h", "z")), part, r1)
    gt = gt + pair(gt)
    gt_other = lax.ppermute(gt, "l", [(0, 1), (1, 0)])
    pieces = exchange(mine + pair(other), ("y", "h", "z", "l"))
    factor_t, piece = scaled(gt, gt_other, zt, pieces, scale_t)
    piece = exchange(piece, ("y", "h", "z", "l"))
    core = joined(core_id, piece, pair(piece))
    return factor_x.T, factor_y.T, factor_t.T, core


def solution(mesh):
    fine = Mesh(mesh.devices.reshape(4, 2, 4, 2, 2), ("y", "h", "z", "l", "c"))
    gx, gy, ta = ("y", "h"), "z", ("l", "c")
    in_specs = (P(gx, gy, ta), P(gy, None), P(ta, None), P(), P(), P())
    out_specs = (P(gx, None), P(gy, None), P(ta, None), P())
    return jax.shard_map(
        on_device, mesh=fine, in_specs=in_specs, out_specs=out_specs, check_vma=False
    )
```

profile of v0, /device:TPU:1, one launch (start us, length us, event | category | flops | bytes accessed | tf_op | source)
XLA Modules:
  0.0 154.8 jit_solution(4506669083661491501)
XLA Ops:
  0.6 0.0 copy-start.2
  0.6 12.2 %shard_map.93 = (bf16[32,256,256]{2,1,0:T(8,128)(2,1)}, f32[64,128]{1,0:T(8,128)}) custom-call(f32[128,256,128]{2,1,0:T(8,128)} %field.3, f32[32,128]{1,0:T(8,128)} %bitcast.17, f32[64,256]{1,0:T(8,128)} %bitcast.15, f32[64,2048]{1,0:T(8,128)} %bitcast.12), custom_call_target="tpu_custom_call" | custom-call | flops 1073741824 | bytes 16777216 | tf_op jit(solution)/shard_map/pallas_call | solution.py:150
  12.9 1.5 collective-permute-start
  14.4 1.1 collective-permute-done
  15.5 0.8 add.12
  16.2 12.6 %all_to_all.35.parts = f32[8,64,128]{2,1,0:T(8,128)S(1)} all-to-all(f32[8,64,128]{2,1,0:T(8,128)S(1)} %broadcast_in_dim.7), channel_id=1, replica_groups=mesh['y'=4,'h'=2,'z'=4,'l'=2,'c'=2] {'z','l'}, dimensions={0} | all-to-all | bytes 524288 | tf_op jit(solution)/shard_map/all_to_all | solution.py:486
  28.8 0.9 shard_map.94
  29.7 0.0 copy-start.4
  29.7 0.6 copy-done.4
  30.4 6.3 %all-to-all-start.1 = ((f32[8,32,128]{2,1,0:T(8,128)}), f32[8,32,128]{2,1,0:T(8,128)S(1)}, u32[]{:S(2)}, u32[]{:S(2)}) async-start(f32[8,32,128]{2,1,0:T(8,128)} %get-tuple-element.26), calls=%async_computation.1 | async-start | bytes 262144 | tf_op jit(solution)/shard_map/all_to_all | solution.py:486
  36.7 0.0 copy-done.2
  36.7 1.1 shard_map.95.a_3_
  37.8 0.0 copy-start
  37.8 1.0 copy-done
  38.8 4.9 %all-to-all-done.1.a_1_ = f32[8,32,128]{2,1,0:T(8,128)S(1)} async-done(((f32[8,32,128]{2,1,0:T(8,128)}), f32[8,32,128]{2,1,0:T(8,128)S(1)}, u32[]{:S(2)}, u32[]{:S(2)}) %all-to-all-start.1) | async-done | bytes 131104 | tf_op jit(solution)/shard_map/all_to_all | solution.py:486
  43.8 0.0 copy-start.5
  43.8 0.7 copy-done.5
  44.4 6.2 %shard_map.96 = (f32[64,128]{1,0:T(8,128)}, f32[64,128]{1,0:T(8,128)}, f32[32,256]{1,0:T(8,128)}, f32[32,256]{1,0:T(8,128)}) custom-call(s32[1]{0:T(128)} %bitcast.a_0_.core_id, f32[8,32,128]{2,1,0:T(8,128)} %copy-done.5, f32[64,128]{1,0:T(8,128)} %copy-done.4, bf16[2048,256]{1,0:T(8,128)(2,1)} %copy-done, bf16[32,256,256]{2,1,0:T(8,128)(2,1)} %get-tuple-element.28.a_4_), custom_call_target="tpu_custom_call" | custom-call | tf_op jit(solution)/shard_map/pallas_call | solution.py:254
  50.6 3.0 %collective-permute-start.1 = (f32[32,256]{1,0:T(8,128)}, f32[32,256]{1,0:T(8,128)S(1)}, u32[]{:S(2)}, u32[]{:S(2)}) collective-permute-start(f32[32,256]{1,0:T(8,128)} %get-tuple-element.31), channel_id=1, source_target_pairs={{0,1},{1,0},{2,3},{3,2},{4,5},{5,4},{6,7},{7,6},{8,9},{9,8},{10,11... | collective-permute-start | bytes 98312 | tf_op jit(solution)/shard_map/ppermute | solution.py:482
  53.6 1.1 collective-permute-done.1
  54.7 0.8 add.13
  55.5 0.8 broadcast_in_dim.8
  56.3 3.6 %all-to-all-start.2 = ((f32[16,32,256]{2,1,0:T(8,128)}), f32[16,32,256]{2,1,0:T(8,128)S(1)}, u32[]{:S(2)}, u32[]{:S(2)}) async-start(f32[16,32,256]{2,1,0:T(8,128)} %broadcast_in_dim.8), calls=%async_computation.2 | async-start | bytes 1048576 | tf_op jit(solution)/shard_map/all_to_all | solution.py:486
  59.9 12.2 %shard_map.97.a_3_ = f32[64,256,128]{2,1,0:T(8,128)} custom-call(f32[64,128]{1,0:T(8,128)} %get-tuple-element.32.q, f32[128,256,128]{2,1,0:T(8,128)} %field.3), custom_call_target="tpu_custom_call" | custom-call | flops 2147483648 | bytes 25165824 | tf_op jit(solution)/shard_map/pallas_call | solution.py:314
  72.1 0.0 all-to-all-done.2
  72.1 0.4 collective-permute-start.2
  72.6 0.9 collective-permute-done.2
  73.4 0.3 shard_map.98
  73.7 0.0 copy-start.3
  73.7 0.6 copy-done.3
  74.3 7.5 %all_to_all.36.a_0_ = f32[4,32,128]{2,1,0:T(8,128)} all-to-all(f32[4,32,128]{2,1,0:T(8,128)S(1)} %get-tuple-element.34), channel_id=1, replica_groups=mesh['y'=4,'h'=2,'z'=4,'l'=2,'c'=2] {'z'}, dimensions={0} | all-to-all | bytes 131072 | tf_op jit(solution)/shard_map/all_to_all | solution.py:486
  81.8 11.3 %shard_map.99 = (f32[64,256]{1,0:T(8,128)}, bf16[4096,256]{1,0:T(8,128)(2,1)}, f32[32,32,128]{2,1,0:T(8,128)}) custom-call(f32[4,32,128]{2,1,0:T(8,128)} %all_to_all.36.a_0_, f32[64,256]{1,0:T(8,128)} %copy-done.3, f32[32,4096]{1,0:T(8,128)} %bitcast.13, f32[64,256,128]{2,1,0:T(8,128)} %shard_map.97.a_3_), custom_call_target="tpu_custom_call" | custom-call | tf_op jit(solution)/shard_map/pallas_call | solution.py:376
  93.1 18.3 %all_to_all.37.parts = f32[32,32,128]{2,1,0:T(8,128)S(1)} all-to-all(f32[32,32,128]{2,1,0:T(8,128)} %get-tuple-element.38), channel_id=1, replica_groups=mesh['y'=4,'h'=2,'z'=4,'l'=2,'c'=2] {'y','h','z'}, dimensions={0} | all-to-all | bytes 1048576 | tf_op jit(solution)/shard_map/all_to_all | solution.py:486
  111.4 0.0 copy-start.1
  111.4 1.6 %copy-done.1 = bf16[4096,256]{1,0:T(8,128)(2,1)S(1)} copy-done((bf16[4096,256]{1,0:T(8,128)(2,1)S(1)}, bf16[4096,256]{1,0:T(8,128)(2,1)}, u32[]{:S(2)}) %copy-start.1) | copy-done | bytes 2097176
  113.0 0.9 shard_map.100
  114.0 3.5 %collective-permute-start.5 = (f32[64,8,128]{2,1,0:T(8,128)S(1)}, f32[64,8,128]{2,1,0:T(8,128)S(1)}, u32[]{:S(2)}, u32[]{:S(2)}) collective-permute-start(f32[64,8,128]{2,1,0:T(8,128)S(1)} %get-tuple-element.43), channel_id=1, source_target_pairs={{0,1},{1,0},{2,3},{3,2},{4,5},{5,4},{6,7},{7,6},{8,9},{9,8},{10,11... | collective-permute-start | bytes 786440 | tf_op jit(solution)/shard_map/ppermute | solution.py:482
  117.5 1.2 collective-permute-done.5
  118.6 0.7 add.15
  119.4 4.8 %all-to-all-start.5 = ((f32[64,8,128]{2,1,0:T(8,128)}), f32[64,8,128]{2,1,0:T(8,128)S(1)}, u32[]{:S(2)}, u32[]{:S(2)}) async-start(f32[64,8,128]{2,1,0:T(8,128)} %add.15), calls=%async_computation.5 | async-start | bytes 524288 | tf_op jit(solution)/shard_map/all_to_all | solution.py:486
  124.2 0.5 collective-permute-start.3
  124.7 0.8 collective-permute-done.3
  125.5 1.3 collective-permute-start.4
  126.8 1.8 %collective-permute-done.4.a_1_ = f32[32,32]{1,0:T(8,128)S(1)} collective-permute-done((f32[32,32]{1,0:T(8,128)S(1)}, f32[32,32]{1,0:T(8,128)S(1)}, u32[]{:S(2)}, u32[]{:S(2)}) %collective-permute-start.4) | collective-permute-done | bytes 4128 | tf_op jit(solution)/shard_map/ppermute | solution.py:525
  128.6 5.3 %all-to-all-done.5.a_3_ = f32[64,8,128]{2,1,0:T(8,128)S(1)} async-done(((f32[64,8,128]{2,1,0:T(8,128)}), f32[64,8,128]{2,1,0:T(8,128)S(1)}, u32[]{:S(2)}, u32[]{:S(2)}) %all-to-all-start.5) | async-done | bytes 262176 | tf_op jit(solution)/shard_map/all_to_all | solution.py:486
  133.9 1.6 %shard_map.101 = (f32[32,128]{1,0:T(8,128)}, f32[64,8,128]{2,1,0:T(8,128)S(1)}) custom-call(f32[32,32]{1,0:T(8,128)S(1)} %add.14.a_0_, f32[32,32]{1,0:T(8,128)S(1)} %collective-permute-done.4.a_1_, f32[32,128]{1,0:T(8,128)S(1)} %get-tuple-element.41.a_2_, f32[64,8,128]{2,1,0:T(8,128)S(1)} %all-to-all-done.5.a_3_), custom_call_target="tpu_custom_call" | custom-call | tf_op jit(solution)/shard_map/pallas_call | solution.py:447
  135.5 14.0 %all_to_all.38.own = f32[64,8,128]{2,1,0:T(8,128)S(1)} all-to-all(f32[64,8,128]{2,1,0:T(8,128)S(1)} %get-tuple-element.45), channel_id=1, replica_groups=mesh['y'=4,'h'=2,'z'=4,'l'=2,'c'=2] {'y','h','z','l'}, dimensions={0} | all-to-all | bytes 524288 | tf_op jit(solution)/shard_map/all_to_all | solution.py:486
  149.4 3.0 %collective-permute-start.6 = (f32[64,8,128]{2,1,0:T(8,128)S(1)}, f32[64,8,128]{2,1,0:T(8,128)S(1)}, u32[]{:S(2)}, u32[]{:S(2)}) collective-permute-start(f32[64,8,128]{2,1,0:T(8,128)S(1)} %all_to_all.38.own), channel_id=1, source_target_pairs={{0,1},{1,0},{2,3},{3,2},{4,5},{5,4},{6,7},{7,6},{8,9},{9,8},{10,11... | collective-permute-start | bytes 786440 | tf_op jit(solution)/shard_map/ppermute | solution.py:482
  152.4 1.2 collective-permute-done.6.other
  153.6 1.3 shard_map.102
  (4 shorter events, 0.1 us)
Async XLA Ops:
  0.6 36.1 %copy-start.2 = (f32[2048,64]{0,1:T(8,128)S(1)}, f32[2048,64]{0,1:T(8,128)}, u32[]{:S(2)}) copy-start(f32[2048,64]{0,1:T(8,128)} %param.10) | copy-start | bytes 1572868
  12.9 2.6 %collective-permute-start = (f32[64,128]{1,0:T(8,128)}, f32[64,128]{1,0:T(8,128)S(1)}, u32[]{:S(2)}, u32[]{:S(2)}) collective-permute-start(f32[64,128]{1,0:T(8,128)} %get-tuple-element.25), channel_id=1, source_target_pairs={{0,1},{1,0},{2,3},{3,2},{4,5},{5,4},{6,7},{7,6},{8,9},{9,8},{10,11... | collective-permute-start | bytes 98312 | tf_op jit(solution)/shard_map/ppermute | solution.py:482
  29.7 0.6 copy-start.4
  30.4 13.4 %all-to-all-start.1 = ((f32[8,32,128]{2,1,0:T(8,128)}), f32[8,32,128]{2,1,0:T(8,128)S(1)}, u32[]{:S(2)}, u32[]{:S(2)}) async-start(f32[8,32,128]{2,1,0:T(8,128)} %get-tuple-element.26), calls=%async_computation.1 | async-start | bytes 262144 | tf_op jit(solution)/shard_map/all_to_all | solution.py:486
  37.8 1.0 copy-start
  43.8 0.7 copy-start.5
  50.6 4.1 %collective-permute-start.1 = (f32[32,256]{1,0:T(8,128)}, f32[32,256]{1,0:T(8,128)S(1)}, u32[]{:S(2)}, u32[]{:S(2)}) collective-permute-start(f32[32,256]{1,0:T(8,128)} %get-tuple-element.31), channel_id=1, source_target_pairs={{0,1},{1,0},{2,3},{3,2},{4,5},{5,4},{6,7},{7,6},{8,9},{9,8},{10,11... | collective-permute-start | bytes 98312 | tf_op jit(solution)/shard_map/ppermute | solution.py:482
  56.3 15.8 %all-to-all-start.2 = ((f32[16,32,256]{2,1,0:T(8,128)}), f32[16,32,256]{2,1,0:T(8,128)S(1)}, u32[]{:S(2)}, u32[]{:S(2)}) async-start(f32[16,32,256]{2,1,0:T(8,128)} %broadcast_in_dim.8), calls=%async_computation.2 | async-start | bytes 1048576 | tf_op jit(solution)/shard_map/all_to_all | solution.py:486
  72.1 1.3 collective-permute-start.2
  73.7 0.6 copy-start.3
  111.4 1.6 %copy-start.1 = (bf16[4096,256]{1,0:T(8,128)(2,1)S(1)}, bf16[4096,256]{1,0:T(8,128)(2,1)}, u32[]{:S(2)}) copy-start(bf16[4096,256]{1,0:T(8,128)(2,1)} %get-tuple-element.39.part) | copy-start | bytes 6291460
  114.0 4.7 %collective-permute-start.5 = (f32[64,8,128]{2,1,0:T(8,128)S(1)}, f32[64,8,128]{2,1,0:T(8,128)S(1)}, u32[]{:S(2)}, u32[]{:S(2)}) collective-permute-start(f32[64,8,128]{2,1,0:T(8,128)S(1)} %get-tuple-element.43), channel_id=1, source_target_pairs={{0,1},{1,0},{2,3},{3,2},{4,5},{5,4},{6,7},{7,6},{8,9},{9,8},{10,11... | collective-permute-start | bytes 786440 | tf_op jit(solution)/shard_map/ppermute | solution.py:482
  119.4 14.5 %all-to-all-start.5 = ((f32[64,8,128]{2,1,0:T(8,128)}), f32[64,8,128]{2,1,0:T(8,128)S(1)}, u32[]{:S(2)}, u32[]{:S(2)}) async-start(f32[64,8,128]{2,1,0:T(8,128)} %add.15), calls=%async_computation.5 | async-start | bytes 524288 | tf_op jit(solution)/shard_map/all_to_all | solution.py:486
  124.2 1.3 collective-permute-start.3
  125.5 3.1 %collective-permute-start.4 = (f32[32,32]{1,0:T(8,128)S(1)}, f32[32,32]{1,0:T(8,128)S(1)}, u32[]{:S(2)}, u32[]{:S(2)}) collective-permute-start(f32[32,32]{1,0:T(8,128)S(1)} %add.14.a_0_), channel_id=1, source_target_pairs={{0,2},{2,0},{1,3},{3,1},{4,6},{6,4},{5,7},{7,5},{8,10},{10,8},{9,1... | collective-permute-start | bytes 12296 | tf_op jit(solution)/shard_map/ppermute | solution.py:525
  149.4 4.2 %collective-permute-start.6 = (f32[64,8,128]{2,1,0:T(8,128)S(1)}, f32[64,8,128]{2,1,0:T(8,128)S(1)}, u32[]{:S(2)}, u32[]{:S(2)}) collective-permute-start(f32[64,8,128]{2,1,0:T(8,128)S(1)} %all_to_all.38.own), channel_id=1, source_target_pairs={{0,1},{1,0},{2,3},{3,2},{4,5},{5,4},{6,7},{7,6},{8,9},{9,8},{10,11... | collective-permute-start | bytes 786440 | tf_op jit(solution)/shard_map/ppermute | solution.py:482
where the time goes:
time: 156 us; the launch traced here: 155 us
  blocking collectives  52.3 us (34%)
  Pallas kernels  48 us (31%)
  starting transfers between devices  27.9 us (18%)
  waiting for transfers between devices  18.2 us (12%)
  local copies, waits for them, and re-layouts  5.33 us (3%)
  other arithmetic  2.31 us (1%)
    all_to_all x4, blocking collectives, exchange(): return lax.all_to_all(x, axes, 0, 0)  52.3 us
    all_to_all x3, starting transfers between devices, exchange(): return lax.all_to_all(x, axes, 0, 0)  14.7 us
    pallas_call x1, Pallas kernels, first(): pl.pallas_call(first_kernel, in_specs=[HBM, VMEM, VMEM, VMEM], out_specs=...  12.2 us
    pallas_call x1, Pallas kernels, contract_x(): pl.pallas_call(contract_x_kernel, in_specs=[VMEM, HBM], out_specs=HBM, ou...  12.2 us
    ppermute x6, starting transfers between devices, pair(): return lax.ppermute(x, 'c', [(0, 1), (1, 0)])  11.9 us
    pallas_call x1, Pallas kernels, third(): pl.pallas_call(lambda *a: third_kernel(scale, *a), in_specs=[VMEM, VMEM,...  11.3 us
    all_to_all x3, waiting for transfers between devices, exchange(): return lax.all_to_all(x, axes, 0, 0)  10.2 us
    pallas_call x1, Pallas kernels, second(): pl.pallas_call(lambda *a: second_kernel(scale, *a), in_specs=[SMEM, VMEM,...  6.2 us
  transfers between devices with their start and end apart: 10, of which 9 were waited for; matrix products, arithmetic and copies ran while one was open for 0% of the time, Pallas kernels for 9%

commit v1 on v0

--- a/solution.py
+++ b/solution.py
@@ -13,8 +13,9 @@
 VMEM = pl.BlockSpec(memory_space=pltpu.VMEM)
 HBM = pl.BlockSpec(memory_space=pltpu.HBM)
 SMEM = pl.BlockSpec(memory_space=pltpu.SMEM)
-MOST = 61 * 1024 * 1024
-BIG = 58 * 1024 * 1024
+MOST = 58 * 1024 * 1024
+BIG = 49 * 1024 * 1024
+AHEAD = 4
 MIDDLE = 4 * 1024 * 1024
 
 
@@ -89,10 +90,12 @@
     return jnp.concatenate([g[:, :64], g[:, 64:]], 0)
 
 
-def first_kernel(field, init_t, init_y, sketch, w, z, held, pair_w, lhs, turned, proj, sems, out_sems):
+def first_kernel(
+    field, init_t, init_y, sketch, w, z, held, pair_w, in_t, in_y, in_s, lhs, unfolded, sems, out_sems
+):
     nx, ny, nt = held.shape
     r3, r2, k = init_t.shape[0], init_y.shape[0], sketch.shape[0]
-    chunks = sems.shape[0]
+    chunks = out_sems.shape[0]
     rows = nx // chunks
 
     def copy(i):
@@ -101,23 +104,29 @@
 
     def copy_out(i, part):
         s = pl.ds(pl.multiple_of(i * rows + part * nx, 16), rows)
-        return pltpu.make_async_copy(pair_w.at[:, s, :], w.at[:, s, :], out_sems.at[i, part])
-
-    for i in range(chunks):
+        return pltpu.make_async_copy(
+            pair_w.at[:, s, :], w.at[pl.ds(0, r3), s, :], out_sems.at[i, part]
+        )
+
+    small = [
+        pltpu.make_async_copy(init_t, in_t, sems.at[chunks]),
+        pltpu.make_async_copy(init_y, in_y, sems.at[chunks + 1]),
+        pltpu.make_async_copy(sketch, in_s, sems.at[chunks + 2]),
+    ]
+    for c in small:
+        c.start()
+    for i in range(AHEAD):
         copy(i).start()
-    lhs[...] = twice(init_t[...])
-    for i in range(0, r2 * r3, 128):
-        turned[i : i + 128, :] = sketch[:, i : i + 128].T
-    hi, lo = split(init_y[...])
-    rhs = jnp.concatenate([hi, hi, lo, lo], 0)
-    for c in range(r3):
-        hi, lo = split(turned[pl.ds(c, r2, stride=r3), :].T)
-        hi, lo = split(dot(jnp.concatenate([hi, lo, hi, lo], 1), rhs))
-        proj[c, :k, :] = hi
-        proj[c, k:, :] = lo
+    small[0].wait()
+    lhs[...] = twice(in_t[...])
 
     def chunk(i, _):
         copy(i).wait()
+
+        @pl.when(i + AHEAD < chunks)
+        def _():
+            copy(i + AHEAD).start()
+
         groups = []
         for x8 in range(0, rows, 8):
             outs = []
@@ -135,62 +144,80 @@
         return 0
 
     lax.fori_loop(0, chunks, chunk, 0)
-    acc = dot(proj[0], pair_w[0], 1, 1)
-    for c in range(1, r3):
-        acc += dot(proj[c], pair_w[c], 1, 1)
-    z[...] = (acc[k:, :nx] + acc[:k, nx:] + acc[k:, nx:]) + acc[:k, :nx]
+    small[1].wait()
+    small[2].wait()
+    hi, lo = split(in_y[...])
+    left = jnp.concatenate([hi, lo], 0)
+    for c8 in range(0, r3, 8):
+        outs = []
+        for c in range(c8, c8 + 8):
+            o = dot(left, pair_w[c], 1, 1)
+            outs.append((o[r2:, :nx] + o[:r2, nx:] + o[r2:, nx:]) + o[:r2, :nx])
+        unfolded[:, c8 : c8 + 8, :] = jnp.swapaxes(jnp.stack(outs, 0), 0, 1)
+    acc = None
+    for a in range(0, r2, 8):
+        hi, lo = split(unfolded[a : a + 8].reshape(8 * r3, nx))
+        sh, sl = split(in_s[:, a * r3 : (a + 8) * r3])
+        o = dot(jnp.concatenate([sh, sl], 0), jnp.concatenate([hi, lo], 1))
+        acc = o if acc is None else acc + o
+    total = (acc[k:, :nx] + acc[:k, nx:] + acc[k:, nx:]) + acc[:k, :nx]
+    for i in range(z.shape[0]):
+        z[i] = total
     for i in range(chunks):
         copy_out(i, 0).wait()
         copy_out(i, 1).wait()
 
 
-def first(field, init_t, init_y, sketch):
+def first(field, init_t, init_y, sketch, copies):
     nx, ny, nt = field.shape
     r3, r2, k = init_t.shape[0], init_y.shape[0], sketch.shape[0]
     return pl.pallas_call(
         first_kernel,
-        in_specs=[HBM, VMEM, VMEM, VMEM],
+        in_specs=[HBM, HBM, HBM, HBM],
         out_specs=[HBM, VMEM],
         out_shape=[
-            jax.ShapeDtypeStruct((r3, 2 * nx, ny), BF16),
-            jax.ShapeDtypeStruct((k, nx), F32),
+            jax.ShapeDtypeStruct((4 * r3, 2 * nx, ny), BF16),
+            jax.ShapeDtypeStruct((copies, k, nx), F32),
         ],
         scratch_shapes=[
             pltpu.VMEM((nx, ny, nt), F32),
             pltpu.VMEM((r3, 2 * nx, ny), BF16),
+            pltpu.VMEM(init_t.shape, F32),
+            pltpu.VMEM(init_y.shape, F32),
+            pltpu.VMEM(sketch.shape, F32),
             pltpu.VMEM((2 * r3, 2 * nt), BF16),
-            pltpu.VMEM((r2 * r3, k), F32),
-            pltpu.VMEM((r3, 2 * k, ny), BF16),
-            pltpu.SemaphoreType.DMA((8,)),
+            pltpu.VMEM((r2, r3, nx), F32),
+            pltpu.SemaphoreType.DMA((11,)),
             pltpu.SemaphoreType.DMA((8, 2)),
         ],
-        compiler_params=room(BIG),
+        compiler_params=room(MOST),
         cost_estimate=pl.CostEstimate(
             flops=8 * nx * ny * nt * r3, bytes_accessed=nx * ny * nt * 4, transcendentals=0
         ),
     )(field, init_t, init_y, sketch)
 
 
-def gram_kernel(parts, z, gram):
-    total = tree_sum([parts[i] for i in range(parts.shape[0])])
+def gram_kernel(*refs):
+    *parts, z, gram = refs
+    total = sum(tree_sum([p[i] for i in range(p.shape[0])]) for p in parts)
     z[...] = total
     g = fold(dot(total, total, 1, 1, HIGH))
     for i in range(gram.shape[0]):
         gram[i] = g
 
 
-def gram_of(parts, copies):
-    k, n = parts.shape[1:]
+def gram_of(copies, *parts):
+    k, n = parts[0].shape[1:]
     return pl.pallas_call(
         gram_kernel,
-        in_specs=[VMEM],
+        in_specs=[VMEM] * len(parts),
         out_specs=[VMEM, VMEM],
         out_shape=[
             jax.ShapeDtypeStruct((k, n), F32),
             jax.ShapeDtypeStruct((copies, k * k // 128, 128), F32),
         ],
         compiler_params=room(MIDDLE),
-    )(parts)
+    )(*parts)
 
 
 def sketch_y_kernel(sketch, out, turned):
@@ -225,8 +252,11 @@
         s = pl.ds(i * each, each)
         return pltpu.make_async_copy(w.at[s], pair_w.at[s], sems.at[i])
 
-    for i in range(r3 // each):
+    def start(i, _):
         copy(i).start()
+        return 0
+
+    lax.fori_loop(0, r3 // each, start, 0)
     g = unfold(tree_sum([grams[i] for i in range(grams.shape[0])]))
     qv = dot(cholesky_inverse(g), z[...], 1, 0, HIGH)
     q[...] = qv
@@ -247,9 +277,9 @@
     other[...] = jnp.where(first, zy[half:], zy[:half])
 
 
-def second(core_id, grams, z, sk, pair_w, scale):
+def second(core_id, grams, z, sk, w, scale, r3):
     r1, nx = z.shape
-    r3, _, ny = pair_w.shape
+    ny = w.shape[2]
     half = jax.ShapeDtypeStruct((sk.shape[0] // r3 // 2, ny), F32)
     return pl.pallas_call(
         lambda *a: second_kernel(scale, *a),
@@ -261,9 +291,12 @@
             half,
             half,
         ],
-        scratch_shapes=[pltpu.VMEM(pair_w.shape, BF16), pltpu.SemaphoreType.DMA((4,))],
-        compiler_params=room(MOST),
-    )(core_id, grams, z, sk, pair_w)
+        scratch_shapes=[
+            pltpu.VMEM((r3, 2 * nx, ny), BF16),
+            pltpu.SemaphoreType.DMA((4,)),
+        ],
+        compiler_params=room(BIG),
+    )(core_id, grams, z, sk, w)
 
 
 def contract_x_kernel(q, field, wx, held, out, lhs, sems, out_sems):
@@ -278,14 +311,21 @@
 
     def copy_out(i):
         s = pl.ds(pl.multiple_of(i * rows, 8), rows)
-        return pltpu.make_async_copy(out.at[:, s, :], wx.at[:, s, :], out_sems.at[i])
-
-    for i in range(chunks):
+        return pltpu.make_async_copy(
+            out.at[:, s, :], wx.at[pl.ds(0, r1), s, :], out_sems.at[i]
+        )
+
+    for i in range(AHEAD):
         copy(i).start()
     lhs[...] = twice(q[...])
 
     def chunk(i, _):
         copy(i).wait()
+
+        @pl.when(i + AHEAD < chunks)
+        def _():
+            copy(i + AHEAD).start()
+
         for y8 in range(0, rows, 8):
             at = pl.multiple_of(i * rows + y8, 8)
             f = jnp.swapaxes(held[:, pl.ds(at, 8), :], 0, 1)
@@ -311,17 +351,18 @@
 def contract_x(q, field):
     nx, ny, nt = field.shape
     r1 = q.shape[0]
+    chunks = ny // 32
     return pl.pallas_call(
         contract_x_kernel,
         in_specs=[VMEM, HBM],
         out_specs=HBM,
-        out_shape=jax.ShapeDtypeStruct((r1, ny, nt), F32),
+        out_shape=jax.ShapeDtypeStruct((2 * r1, ny, nt), F32),
         scratch_shapes=[
             pltpu.VMEM((nx, ny, nt), F32),
             pltpu.VMEM((r1, ny, nt), F32),
             pltpu.VMEM((2 * r1, 2 * nx), BF16),
-            pltpu.SemaphoreType.DMA((8,)),
-            pltpu.SemaphoreType.DMA((8,)),
+            pltpu.SemaphoreType.DMA((chunks,)),
+            pltpu.SemaphoreType.DMA((chunks,)),
         ],
         compiler_params=room(BIG),
         cost_estimate=pl.CostEstimate(
@@ -330,7 +371,7 @@
     )(q, field)
 
 
-def third_kernel(scale, grams, z, sketch, w_hbm, factor, part, zt, wx, sems):
+def third_kernel(scale, g0, g1, g2, g3, z, sketch, wa, factor, part, zt, wx, sems):
     r1, ny, nt = wx.shape
     r2 = z.shape[0]
     chunks = sems.shape[0]
@@ -338,142 +379,159 @@
 
     def copy(i):
         s = pl.ds(i * rows, rows)
-        return pltpu.make_async_copy(w_hbm.at[s], wx.at[s], sems.at[i])
-
-    for i in range(chunks):
+        return pltpu.make_async_copy(wa.at[s], wx.at[s], sems.at[i])
+
+    def start(i, _):
         copy(i).start()
-    g = unfold(tree_sum([grams[i] for i in range(grams.shape[0])]))
+        return 0
+
+    lax.fori_loop(0, chunks, start, 0)
+    g = unfold((g0[...] + g1[...]) + (g2[...] + g3[...]))
     qv = dot(cholesky_inverse(g), z[...], 1, 0, HIGH)
     factor[...] = qv * scale
     hi, lo = split(qv)
     lhs = jnp.concatenate([hi, lo], 0)
     k = sketch.shape[0]
-    group = rows
+    group = 4
 
     def step(i, acc):
         copy(i).wait()
-        for b in range(group):
-            hi, lo = split(wx[i * group + b])
+        for b in range(rows):
+            hi, lo = split(wx[i * rows + b])
             o = dot(lhs, jnp.concatenate([hi, lo], 1))
             o = (o[r2:, :nt] + o[:r2, nt:] + o[r2:, nt:]) + o[:r2, :nt]
             hi, lo = split(o)
-            at = pl.multiple_of(i * group * r2 + b * r2, r2)
+            at = pl.multiple_of((i * rows + b) * r2, r2)
             part[pl.ds(at, r2), :] = jnp.concatenate([hi, lo], 1)
-        s = pl.ds(pl.multiple_of(i * group * r2, group * r2), group * r2)
-        hi, lo = split(sketch[:, s])
-        return acc + dot(jnp.concatenate([hi, lo], 0), part[s, :])
-
-    acc = lax.fori_loop(0, r1 // group, step, jnp.zeros((2 * k, 2 * nt), F32))
+        for b in range(0, rows, group):
+            n = group * r2
+            s = pl.ds(pl.multiple_of((i * rows + b) * r2, n), n)
+            hi, lo = split(sketch[:, s])
+            acc = acc + dot(jnp.concatenate([hi, lo], 0), part[s, :])
+        return acc
+
+    acc = jnp.zeros((2 * k, 2 * nt), F32)
+    for i in range(chunks):
+        acc = step(i, acc)
     total = (acc[k:, :nt] + acc[:k, nt:] + acc[k:, nt:]) + acc[:k, :nt]
     for i in range(zt.shape[0]):
         zt[i] = total
 
 
-def third(grams, z, sketch, wx, scale, copies):
+def third(grams, z, sketch, wa, scale, copies, r1):
     r2, ny = z.shape
-    r1, _, nt = wx.shape
+    nt = wa.shape[2]
     k = sketch.shape[0]
     return pl.pallas_call(
         lambda *a: third_kernel(scale, *a),
-        in_specs=[VMEM, VMEM, VMEM, HBM],
+        in_specs=[VMEM] * 6 + [HBM],
         out_specs=[VMEM] * 3,
         out_shape=[
             jax.ShapeDtypeStruct((r2, ny), F32),
             jax.ShapeDtypeStruct((r1 * r2, 2 * nt), BF16),
             jax.ShapeDtypeStruct((copies, k, nt), F32),
         ],
-        scratch_shapes=[pltpu.VMEM(wx.shape, F32), pltpu.SemaphoreType.DMA((16,))],
+        scratch_shapes=[pltpu.VMEM((r1, ny, nt), F32), pltpu.SemaphoreType.DMA((2,))],
         compiler_params=room(BIG),
-    )(grams, z, sketch, wx)
-
-
-def core_kernel(core_id, parts, part, z, gram, mine, other):
+    )(*grams, z, sketch, wa)
+
+
+def core_kernel(parts, part, z, gram, out):
     total = tree_sum([parts[i] for i in range(parts.shape[0])])
     z[...] = total
     gram[...] = dot(total, total, 1, 1, HIGH)
     k = total.shape[0]
     lhs = twice(total)
     group = lax.broadcasted_iota(jnp.int32, (8, 128), 1) // 32
-    first = core_id[0] == 0
     for i in range(part.shape[0] // 256):
         o = dot(lhs, part[i * 256 : (i + 1) * 256, :], 1, 1)
         o = o[k:] + o[:k]
         for j in range(2):
             v = [o[8 * g : 8 * g + 8, 128 * j : 128 * j + 128] for g in range(4)]
-            slots = []
             for s in range(4):
                 t = None
                 for g in range(4):
                     shift = (g - s) * 32 % 128
                     u = pltpu.roll(v[g], shift, 1) if shift else v[g]
                     t = u if t is None else jnp.where(group == g, u, t)
-                slots.append(t)
-            for b in range(2):
-                at = i * 4 + j * 2 + b
-                mine[at] = jnp.where(first, slots[2 * b], slots[2 * b + 1])
-                other[at] = jnp.where(first, slots[2 * b + 1], slots[2 * b])
-
-
-def core_terms(core_id, parts, part, r1):
+                at = i * 4 + j * 2 + s // 2
+                out[at, 8 * (s % 2) : 8 * (s % 2) + 8, :] = t
+
+
+def core_terms(parts, part, r1):
     k, nt = parts.shape[1:]
-    slots = jax.ShapeDtypeStruct((r1, 8, 128), F32)
     return pl.pallas_call(
         core_kernel,
-        in_specs=[SMEM, VMEM, VMEM],
-        out_specs=[VMEM] * 4,
+        in_specs=[VMEM, VMEM],
+        out_specs=[VMEM] * 3,
         out_shape=[
             jax.ShapeDtypeStruct((k, nt), F32),
             jax.ShapeDtypeStruct((k, k), F32),
-            slots,
-            slots,
+            jax.ShapeDtypeStruct((r1, 16, 128), F32),
         ],
         compiler_params=room(MIDDLE),
-    )(core_id, parts, part)
-
-
-def scale_kernel(scale, gram0, gram1, z, pieces, factor, out, held):
-    inv = cholesky_inverse(gram0[...] + gram1[...])
-    factor[...] = dot(inv, z[...], 1, 0, HIGH) * scale
-    piece = tree_sum([pieces[i] for i in range(pieces.shape[0])])
+    )(parts, part)
+
+
+def inverse_kernel(scale, g0, g1, g2, g3, z, factor, inv):
+    inv[...] = cholesky_inverse((g0[...] + g1[...]) + (g2[...] + g3[...]))
+    factor[...] = dot(inv[...], z[...], 1, 0, HIGH) * scale
+
+
+def last_factor(grams, z, scale):
+    k, nt = z.shape
+    return pl.pallas_call(
+        lambda *a: inverse_kernel(scale, *a),
+        in_specs=[VMEM] * 5,
+        out_specs=[VMEM] * 2,
+        out_shape=[jax.ShapeDtypeStruct((k, nt), F32), jax.ShapeDtypeStruct((k, k), F32)],
+        compiler_params=room(MIDDLE),
+        cost_estimate=pl.CostEstimate(flops=10**7, bytes_accessed=2 * 10**6, transcendentals=0),
+    )(*grams, z)
+
+
+def scale_kernel(core_id, inv, own, other, out, held):
+    piece = own[...] + other[...]
+    piece = jnp.where(core_id[0] == 0, piece[:8], piece[8:])
     x = jnp.concatenate([piece[:, 32 * g : 32 * g + 32] for g in range(4)], 0)
-    held[...] = dot(x, inv, 0, 1, HIGH)
+    held[...] = dot(x, inv[...], 0, 1, HIGH)
     row = jnp.concatenate([held[pl.ds(s, 8, stride=4), :] for s in range(4)], 1)
     for i in range(out.shape[0]):
         out[i] = row
 
 
-def scaled(gram0, gram1, z, pieces, scale):
-    k, nt = z.shape
-    return pl.pallas_call(
-        lambda *a: scale_kernel(scale, *a),
-        in_specs=[VMEM] * 4,
-        out_specs=[VMEM] * 2,
-        out_shape=[
-            jax.ShapeDtypeStruct((k, nt), F32),
-            jax.ShapeDtypeStruct(pieces.shape, F32),
-        ],
+def scaled(core_id, inv, own, other, copies):
+    k = inv.shape[0]
+    return pl.pallas_call(
+        scale_kernel,
+        in_specs=[SMEM] + [VMEM] * 3,
+        out_specs=VMEM,
+        out_shape=jax.ShapeDtypeStruct((copies, 8, 128), F32),
         scratch_shapes=[pltpu.VMEM((k, k), F32)],
         compiler_params=room(MIDDLE),
-    )(gram0, gram1, z, pieces)
+    )(core_id, inv, own, other)
 
 
 def join_kernel(core_id, own, other, out):
+    n, rows, _ = own.shape
     first = core_id[0] == 0
-    half = out.shape[1] // 2
-    for r in range(own.shape[1]):
-        a = own[:, r, :]
-        b = other[:, r, :]
-        out[:, r * 128 : (r + 1) * 128] = jnp.where(first, a, b)
-        out[:, half + r * 128 : half + (r + 1) * 128] = jnp.where(first, b, a)
+    half = rows * 128
+    for b in range(0, n, 8):
+        x = jnp.swapaxes(own[b : b + 8], 0, 1)
+        y = jnp.swapaxes(other[b : b + 8], 0, 1)
+        for r in range(rows):
+            at = r * 128
+            out[b : b + 8, at : at + 128] = jnp.where(first, x[r], y[r])
+            out[b : b + 8, half + at : half + at + 128] = jnp.where(first, y[r], x[r])
 
 
 def joined(core_id, own, other):
-    n = own.shape[0]
+    n, rows, _ = own.shape
     return pl.pallas_call(
         join_kernel,
         in_specs=[SMEM, VMEM, VMEM],
         out_specs=VMEM,
-        out_shape=jax.ShapeDtypeStruct((n, 2 * 8 * 128), F32),
+        out_shape=jax.ShapeDtypeStruct((n, 2 * rows * 128), F32),
         compiler_params=room(MIDDLE),
     )(core_id, own, other)
 
@@ -484,6 +542,10 @@
 
 def exchange(x, axes):
     return lax.all_to_all(x, axes, 0, 0)
+
+
+def of_four(x, axes):
+    return [x] + [lax.ppermute(x, axes, [(i, i ^ s) for i in range(4)]) for s in (1, 2, 3)]
 
 
 def spread(x, axes):
@@ -508,25 +570,24 @@
     scale_t = math.sqrt(rows_t * lax.axis_size(("l", "c")))
     core_id = lax.axis_index("c").astype(jnp.int32).reshape(1)
 
-    pair_w, zx = first(field, init_t.T, init_y.T, sketch_x.T)
-    zx, gx = gram_of(spread(zx + pair(zx), ("z", "l")), 8)
+    w, zx = first(field, init_t.T, init_y.T, sketch_x.T, 8)
+    zx = exchange(zx, ("z", "l"))
+    zx, gx = gram_of(8, zx, pair(zx))
     sk_y = prepared_y(sketch_y.T, r3)
     qx, factor_x, mine, other = second(
-        core_id, exchange(gx, ("y", "h")), zx, sk_y, pair_w, scale_x
+        core_id, exchange(gx, ("y", "h")), zx, sk_y, w, scale_x, r3
     )
     wx = contract_x(qx, field)
     zy = spread(mine + pair(other), ("y", "h", "l")).sum(0)
     zy, wx = lax.optimization_barrier((zy, wx))
-    zy = both(zy, 0)
-    zy, gy = gram_of(zy[None], 4)
-    factor_y, part, zt = third(exchange(gy, ("z",)), zy, sketch_t.T, wx, scale_y, 32)
-    zt, gt, mine, other = core_terms(core_id, exchange(zt, ("y", "h", "z")), part, r1)
-    gt = gt + pair(gt)
-    gt_other = lax.ppermute(gt, "l", [(0, 1), (1, 0)])
-    pieces = exchange(mine + pair(other), ("y", "h", "z", "l"))
-    factor_t, piece = scaled(gt, gt_other, zt, pieces, scale_t)
-    piece = exchange(piece, ("y", "h", "z", "l"))
-    core = joined(core_id, piece, pair(piece))
+    zy, gy = gram_of(1, both(zy, 0)[None])
+    factor_y, part, zt = third(of_four(gy[0], "z"), zy, sketch_t.T, wx, scale_y, 32, r1)
+    zt, gt, core = core_terms(exchange(zt, ("y", "h", "z")), part, r1)
+    factor_t, inv_t = last_factor(of_four(gt, ("l", "c")), zt, scale_t)
+    chips = ("y", "h", "z", "l")
+    piece, inv_t = lax.optimization_barrier((exchange(core, chips).sum(0), inv_t))
+    core = exchange(scaled(core_id, inv_t, piece, pair(piece), r1), chips)
+    core = joined(core_id, core, pair(core))
     return factor_x.T, factor_y.T, factor_t.T, core
 
 

time: 156 us -> 140 us (0.90)
  Pallas kernels: 48 us -> 39.9 us
  starting transfers between devices: 27.9 us -> 34.1 us
  blocking collectives: 52.3 us -> 47.1 us
  local copies, waits for them, and re-layouts: 5.33 us -> 0.86 us
  other arithmetic: 2.31 us -> 0.12 us
  waiting for transfers between devices: 18.2 us -> 16.6 us
    ppermute x1 -> x6, starting transfers between devices: 1.29 us -> 8.31 us  [of_four(): lax.ppermute(x, axes, [(i, i ^ s) for i in range(4)])]
    pallas_call x6 -> x7, Pallas kernels: 27.2 us -> 21.8 us  [the longest x1 11.9 us: first(): pl.pallas_call(first_kernel, in_specs=[HBM, HBM, HBM, HBM], out_specs=[HB...]
    all_to_all x4 -> x3, blocking collectives: 52.3 us -> 47.1 us  [exchange(): return lax.all_to_all(x, axes, 0, 0)]
    unnamed x12 -> x4, local copies, waits for them, and re-layouts: 4.47 us -> 0.01 us
    all_to_all x3, waiting for transfers between devices: 10.2 us -> 5.92 us  [exchange(): return lax.all_to_all(x, axes, 0, 0)]
    ppermute x1 -> x6, waiting for transfers between devices: 1.77 us -> 5.79 us  [of_four(): lax.ppermute(x, axes, [(i, i ^ s) for i in range(4)])]
    pallas_call x1, Pallas kernels: 6.2 us -> 4.5 us  [second(): pl.pallas_call(lambda *a: second_kernel(scale, *a), in_specs=[SMEM, VMEM,...]
    ppermute x6 -> x5, waiting for transfers between devices: 6.16 us -> 4.87 us  [pair(): return lax.ppermute(x, 'c', [(0, 1), (1, 0)])]
  transfers between devices with their start and end apart: 10 -> 14, of which waited for: 9 -> 10; matrix products, arithmetic and copies ran while one was open for 0% -> 0% of each run, Pallas kernels for 9% -> 10%
where the time goes in v1:
time: 140 us; the launch traced here: 139 us
  blocking collectives  47.1 us (34%)
  Pallas kernels  39.9 us (28%)
  starting transfers between devices  34.1 us (24%)
  waiting for transfers between devices  16.6 us (12%)
    all_to_all x3, blocking collectives, exchange(): return lax.all_to_all(x, axes, 0, 0)  47.1 us
    all_to_all x3, starting transfers between devices, exchange(): return lax.all_to_all(x, axes, 0, 0)  14.6 us
    pallas_call x1, Pallas kernels, first(): pl.pallas_call(first_kernel, in_specs=[HBM, HBM, HBM, HBM], out_specs=[HB...  11.9 us
    pallas_call x1, Pallas kernels, contract_x(): pl.pallas_call(contract_x_kernel, in_specs=[VMEM, HBM], out_specs=HBM, ou...  11.5 us
    ppermute x5, starting transfers between devices, pair(): return lax.ppermute(x, 'c', [(0, 1), (1, 0)])  11.2 us
    ppermute x6, starting transfers between devices, of_four(): lax.ppermute(x, axes, [(i, i ^ s) for i in range(4)])  8.31 us
    all_to_all x3, waiting for transfers between devices, exchange(): return lax.all_to_all(x, axes, 0, 0)  5.92 us
    ppermute x6, waiting for transfers between devices, of_four(): lax.ppermute(x, axes, [(i, i ^ s) for i in range(4)])  5.79 us
  transfers between devices with their start and end apart: 14, of which 10 were waited for; matrix products, arithmetic and copies ran while one was open for 0% of the time, Pallas kernels for 10%

profile of v1, /device:TPU:1, one launch (start us, length us, event | category | flops | bytes accessed | tf_op | source)
XLA Modules:
  0.0 139.4 jit_solution(8857209825157466805)
XLA Ops:
  0.6 0.0 copy-start
  0.6 11.9 %shard_map.93 = (bf16[128,256,256]{2,1,0:T(8,128)(2,1)}, f32[8,64,128]{2,1,0:T(8,128)}) custom-call(f32[128,256,128]{2,1,0:T(8,128)} %field.3, f32[32,128]{1,0:T(8,128)} %bitcast.22, f32[64,256]{1,0:T(8,128)} %bitcast.20, f32[64,2048]{1,0:T(8,128)} %bitcast.18), custom_call_target="tpu_custom_call" | custom-call | flops 1073741824 | bytes 16777216 | tf_op jit(solution)/shard_map/pallas_call | solution.py:174
  12.6 13.0 %all_to_all.30.refs_0_ = f32[8,64,128]{2,1,0:T(8,128)S(1)} all-to-all(f32[8,64,128]{2,1,0:T(8,128)} %get-tuple-element.26), channel_id=1, replica_groups=mesh['y'=4,'h'=2,'z'=4,'l'=2,'c'=2] {'z','l'}, dimensions={0} | all-to-all | bytes 524288 | tf_op jit(solution)/shard_map/all_to_all | solution.py:544
  25.6 2.1 %collective-permute-start = (f32[8,64,128]{2,1,0:T(8,128)S(1)}, f32[8,64,128]{2,1,0:T(8,128)S(1)}, u32[]{:S(2)}, u32[]{:S(2)}) collective-permute-start(f32[8,64,128]{2,1,0:T(8,128)S(1)} %all_to_all.30.refs_0_), channel_id=1, source_target_pairs={{0,1},{1,0},{2,3},{3,2},{4,5},{5,4},{6,7},{7,6},{8,9},{9,8},{10,11... | collective-permute-start | bytes 786440 | tf_op jit(solution)/shard_map/ppermute | solution.py:540
  27.6 1.2 collective-permute-done.refs_1_
  28.8 0.9 shard_map.94
  29.7 6.4 %all-to-all-start.1 = ((f32[8,32,128]{2,1,0:T(8,128)}), f32[8,32,128]{2,1,0:T(8,128)S(1)}, u32[]{:S(2)}, u32[]{:S(2)}) async-start(f32[8,32,128]{2,1,0:T(8,128)} %get-tuple-element.27), calls=%async_computation.1 | async-start | bytes 262144 | tf_op jit(solution)/shard_map/all_to_all | solution.py:544
  36.1 0.0 copy-done
  36.1 1.1 shard_map.95.a_3_
  37.2 5.9 %all-to-all-done.1.a_1_ = f32[8,32,128]{2,1,0:T(8,128)S(1)} async-done(((f32[8,32,128]{2,1,0:T(8,128)}), f32[8,32,128]{2,1,0:T(8,128)S(1)}, u32[]{:S(2)}, u32[]{:S(2)}) %all-to-all-start.1) | async-done | bytes 131104 | tf_op jit(solution)/shard_map/all_to_all | solution.py:544
  43.1 4.5 %shard_map.96 = (f32[64,128]{1,0:T(8,128)S(1)}, f32[64,128]{1,0:T(8,128)}, f32[32,256]{1,0:T(8,128)S(1)}, f32[32,256]{1,0:T(8,128)S(1)}) custom-call(s32[1]{0:T(128)} %bitcast.a_0_.core_id, f32[8,32,128]{2,1,0:T(8,128)S(1)} %all-to-all-done.1.a_1_, f32[64,128]{1,0:T(8,128)S(1)} %get-tuple-element.28.a_2_, bf16[2048,256]{1,0:T(8,128)(2,1)S(1)} %shard_map.95.a_3_, ...), custom_call_target="tpu_custom_call" | custom-call | tf_op jit(solution)/shard_map/pallas_call | solution.py:284
  47.6 1.9 %collective-permute-start.1 = (f32[32,256]{1,0:T(8,128)S(1)}, f32[32,256]{1,0:T(8,128)S(1)}, u32[]{:S(2)}, u32[]{:S(2)}) collective-permute-start(f32[32,256]{1,0:T(8,128)S(1)} %get-tuple-element.32), channel_id=1, source_target_pairs={{0,1},{1,0},{2,3},{3,2},{4,5},{5,4},{6,7},{7,6},{8,9},{9,8},{10,11... | collective-permute-start | bytes 98312 | tf_op jit(solution)/shard_map/ppermute | solution.py:540
  49.5 0.9 collective-permute-done.1
  50.4 0.8 broadcast_in_dim.4
  51.2 3.6 %all-to-all-start.2 = ((f32[16,32,256]{2,1,0:T(8,128)}), f32[16,32,256]{2,1,0:T(8,128)S(1)}, u32[]{:S(2)}, u32[]{:S(2)}) async-start(f32[16,32,256]{2,1,0:T(8,128)} %broadcast_in_dim.4), calls=%async_computation.2 | async-start | bytes 1048576 | tf_op jit(solution)/shard_map/all_to_all | solution.py:544
  54.8 0.0 copy-start.1
  54.8 11.5 %shard_map.97.a_6_ = f32[128,256,128]{2,1,0:T(8,128)} custom-call(f32[64,128]{1,0:T(8,128)S(1)} %get-tuple-element.33.q, f32[128,256,128]{2,1,0:T(8,128)} %field.3), custom_call_target="tpu_custom_call" | custom-call | flops 2147483648 | bytes 25165824 | tf_op jit(solution)/shard_map/pallas_call | solution.py:355
  66.3 0.0 all-to-all-done.2
  66.4 1.0 collective-permute-start.2
  67.4 0.9 collective-permute-done.2
  68.2 0.3 shard_map.98
  68.5 0.7 collective-permute-start.5
  69.2 1.4 collective-permute-start.4
  70.5 1.2 collective-permute-start.3
  71.8 0.5 collective-permute-done.5.a_3_
  72.3 1.0 collective-permute-done.4.a_2_
  73.3 0.1 collective-permute-done.3.a_1_
  73.4 0.0 copy-done.1
  73.4 5.1 %shard_map.99 = (f32[64,256]{1,0:T(8,128)}, bf16[4096,256]{1,0:T(8,128)(2,1)S(1)}, f32[32,32,128]{2,1,0:T(8,128)S(1)}) custom-call(f32[32,128]{1,0:T(8,128)S(1)} %bitcast.17, f32[32,128]{1,0:T(8,128)S(1)} %collective-permute-done.3.a_1_, f32[32,128]{1,0:T(8,128)S(1)} %collective-permute-done.4.a_2_, f32[32,128]{1,0:T(8,128)S(1)} %collective-permute-done.5.a_3_, ...), custom_call_target="tpu_custom_call" | custom-call | tf_op jit(solution)/shard_map/pallas_call | solution.py:425
  78.5 18.9 %all_to_all.31.parts = f32[32,32,128]{2,1,0:T(8,128)S(1)} all-to-all(f32[32,32,128]{2,1,0:T(8,128)S(1)} %get-tuple-element.39), channel_id=1, replica_groups=mesh['y'=4,'h'=2,'z'=4,'l'=2,'c'=2] {'y','h','z'}, dimensions={0} | all-to-all | bytes 1048576 | tf_op jit(solution)/shard_map/all_to_all | solution.py:544
  97.4 1.7 %shard_map.100 = (f32[32,128]{1,0:T(8,128)S(1)}, f32[32,32]{1,0:T(8,128)S(1)}, f32[64,16,128]{2,1,0:T(8,128)}) custom-call(f32[32,32,128]{2,1,0:T(8,128)S(1)} %all_to_all.31.parts, bf16[4096,256]{1,0:T(8,128)(2,1)S(1)} %get-tuple-element.40.part), custom_call_target="tpu_custom_call" | custom-call | tf_op jit(solution)/shard_map/pallas_call | solution.py:463
  99.2 4.6 %all-to-all-start.4 = ((f32[64,16,128]{2,1,0:T(8,128)}), f32[64,16,128]{2,1,0:T(8,128)S(1)}, u32[]{:S(2)}, u32[]{:S(2)}) async-start(f32[64,16,128]{2,1,0:T(8,128)} %get-tuple-element.44), calls=%async_computation.4 | async-start | bytes 1048576 | tf_op jit(solution)/shard_map/all_to_all | solution.py:544
  103.8 4.5 %collective-permute-start.8 = (f32[32,32]{1,0:T(8,128)S(1)}, f32[32,32]{1,0:T(8,128)S(1)}, u32[]{:S(2)}, u32[]{:S(2)}) collective-permute-start(f32[32,32]{1,0:T(8,128)S(1)} %get-tuple-element.41.a_0_), channel_id=1, source_target_pairs={{0,3},{1,2},{2,1},{3,0},{4,7},{5,6},{6,5},{7,4},{8,11},{9,10},{10,... | collective-permute-start | bytes 12296 | tf_op jit(solution)/shard_map/ppermute | solution.py:548
  108.3 0.2 collective-permute-start.7
  108.5 0.3 collective-permute-start.6
  108.8 4.1 %collective-permute-done.8.a_3_ = f32[32,32]{1,0:T(8,128)S(1)} collective-permute-done((f32[32,32]{1,0:T(8,128)S(1)}, f32[32,32]{1,0:T(8,128)S(1)}, u32[]{:S(2)}, u32[]{:S(2)}) %collective-permute-start.8) | collective-permute-done | bytes 4128 | tf_op jit(solution)/shard_map/ppermute | solution.py:548
  113.0 0.0 collective-permute-done.7.a_2_
  113.0 0.0 collective-permute-done.6.a_1_
  113.0 1.6 %shard_map.101 = (f32[32,128]{1,0:T(8,128)}, f32[32,32]{1,0:T(8,128)S(1)}) custom-call(f32[32,32]{1,0:T(8,128)S(1)} %get-tuple-element.41.a_0_, f32[32,32]{1,0:T(8,128)S(1)} %collective-permute-done.6.a_1_, f32[32,32]{1,0:T(8,128)S(1)} %collective-permute-done.7.a_2_, f32[32,32]{1,0:T(8,128)S(1)} %collective-permute-done.8.a_3_, ...), custom_call_target="tpu_custom_call" | custom-call | flops 10000000 | bytes 2000000 | tf_op jit(solution)/shard_map/pallas_call | solution.py:483
  114.5 0.0 all-to-all-done.4
  114.5 0.1 reduce_sum.19.own
  114.6 4.7 %collective-permute-start.9 = (f32[16,128]{1,0:T(8,128)S(1)}, f32[16,128]{1,0:T(8,128)S(1)}, u32[]{:S(2)}, u32[]{:S(2)}) collective-permute-start(f32[16,128]{1,0:T(8,128)S(1)} %reduce_sum.19.own), channel_id=1, source_target_pairs={{0,1},{1,0},{2,3},{3,2},{4,5},{5,4},{6,7},{7,6},{8,9},{9,8},{10,11... | collective-permute-start | bytes 24584 | tf_op jit(solution)/shard_map/ppermute | solution.py:540
  119.3 0.8 collective-permute-done.9.other
  120.1 0.4 shard_map.102
  120.5 15.2 %all_to_all.32.own = f32[64,8,128]{2,1,0:T(8,128)S(1)} all-to-all(f32[64,8,128]{2,1,0:T(8,128)S(1)} %shard_map.102), channel_id=1, replica_groups=mesh['y'=4,'h'=2,'z'=4,'l'=2,'c'=2] {'y','h','z','l'}, dimensions={0} | all-to-all | bytes 524288 | tf_op jit(solution)/shard_map/all_to_all | solution.py:544
  135.7 1.6 %collective-permute-start.10 = (f32[64,8,128]{2,1,0:T(8,128)S(1)}, f32[64,8,128]{2,1,0:T(8,128)S(1)}, u32[]{:S(2)}, u32[]{:S(2)}) collective-permute-start(f32[64,8,128]{2,1,0:T(8,128)S(1)} %all_to_all.32.own), channel_id=1, source_target_pairs={{0,1},{1,0},{2,3},{3,2},{4,5},{5,4},{6,7},{7,6},{8,9},{9,8},{10,11... | collective-permute-start | bytes 786440 | tf_op jit(solution)/shard_map/ppermute | solution.py:540
  137.3 1.2 collective-permute-done.10.other
  138.5 0.9 shard_map.103
  (3 shorter events, 0.0 us)
Async XLA Ops:
  0.6 35.4 %copy-start = (f32[2048,64]{0,1:T(8,128)S(1)}, f32[2048,64]{0,1:T(8,128)}, u32[]{:S(2)}) copy-start(f32[2048,64]{0,1:T(8,128)} %param.10) | copy-start | bytes 1572868
  25.6 3.2 %collective-permute-start = (f32[8,64,128]{2,1,0:T(8,128)S(1)}, f32[8,64,128]{2,1,0:T(8,128)S(1)}, u32[]{:S(2)}, u32[]{:S(2)}) collective-permute-start(f32[8,64,128]{2,1,0:T(8,128)S(1)} %all_to_all.30.refs_0_), channel_id=1, source_target_pairs={{0,1},{1,0},{2,3},{3,2},{4,5},{5,4},{6,7},{7,6},{8,9},{9,8},{10,11... | collective-permute-start | bytes 786440 | tf_op jit(solution)/shard_map/ppermute | solution.py:540
  29.7 13.4 %all-to-all-start.1 = ((f32[8,32,128]{2,1,0:T(8,128)}), f32[8,32,128]{2,1,0:T(8,128)S(1)}, u32[]{:S(2)}, u32[]{:S(2)}) async-start(f32[8,32,128]{2,1,0:T(8,128)} %get-tuple-element.27), calls=%async_computation.1 | async-start | bytes 262144 | tf_op jit(solution)/shard_map/all_to_all | solution.py:544
  47.6 2.7 %collective-permute-start.1 = (f32[32,256]{1,0:T(8,128)S(1)}, f32[32,256]{1,0:T(8,128)S(1)}, u32[]{:S(2)}, u32[]{:S(2)}) collective-permute-start(f32[32,256]{1,0:T(8,128)S(1)} %get-tuple-element.32), channel_id=1, source_target_pairs={{0,1},{1,0},{2,3},{3,2},{4,5},{5,4},{6,7},{7,6},{8,9},{9,8},{10,11... | collective-permute-start | bytes 98312 | tf_op jit(solution)/shard_map/ppermute | solution.py:540
  51.2 15.1 %all-to-all-start.2 = ((f32[16,32,256]{2,1,0:T(8,128)}), f32[16,32,256]{2,1,0:T(8,128)S(1)}, u32[]{:S(2)}, u32[]{:S(2)}) async-start(f32[16,32,256]{2,1,0:T(8,128)} %broadcast_in_dim.4), calls=%async_computation.2 | async-start | bytes 1048576 | tf_op jit(solution)/shard_map/all_to_all | solution.py:544
  54.8 18.6 %copy-start.1 = (f32[4096,32]{0,1:T(8,128)S(1)}, f32[4096,32]{0,1:T(8,128)}, u32[]{:S(2)}) copy-start(f32[4096,32]{0,1:T(8,128)} %param.11) | copy-start | bytes 1572868
  66.4 1.8 %collective-permute-start.2 = (f32[32,256]{1,0:T(8,128)S(1)}, f32[32,256]{1,0:T(8,128)S(1)}, u32[]{:S(2)}, u32[]{:S(2)}) collective-permute-start(f32[32,256]{1,0:T(8,128)S(1)} %reduce_sum.18), channel_id=1, source_target_pairs={{0,1},{1,0},{2,3},{3,2},{4,5},{5,4},{6,7},{7,6},{8,9},{9,8},{10,11... | collective-permute-start | bytes 98312 | tf_op jit(solution)/shard_map/ppermute | solution.py:540
  68.5 3.8 %collective-permute-start.5 = (f32[32,128]{1,0:T(8,128)S(1)}, f32[32,128]{1,0:T(8,128)S(1)}, u32[]{:S(2)}, u32[]{:S(2)}) collective-permute-start(f32[32,128]{1,0:T(8,128)S(1)} %bitcast.14), channel_id=1, source_target_pairs={{0,12},{4,8},{8,4},{12,0},{1,13},{5,9},{9,5},{13,1},{2,14},{6,10},... | collective-permute-start | bytes 49160 | tf_op jit(solution)/shard_map/ppermute | solution.py:548
  69.2 4.2 %collective-permute-start.4 = (f32[32,128]{1,0:T(8,128)S(1)}, f32[32,128]{1,0:T(8,128)S(1)}, u32[]{:S(2)}, u32[]{:S(2)}) collective-permute-start(f32[32,128]{1,0:T(8,128)S(1)} %bitcast.15), channel_id=1, source_target_pairs={{0,8},{4,12},{8,0},{12,4},{1,9},{5,13},{9,1},{13,5},{2,10},{6,14},... | collective-permute-start | bytes 49160 | tf_op jit(solution)/shard_map/ppermute | solution.py:548
  70.5 2.9 %collective-permute-start.3 = (f32[32,128]{1,0:T(8,128)S(1)}, f32[32,128]{1,0:T(8,128)S(1)}, u32[]{:S(2)}, u32[]{:S(2)}) collective-permute-start(f32[32,128]{1,0:T(8,128)S(1)} %bitcast.16), channel_id=1, source_target_pairs={{0,4},{4,0},{8,12},{12,8},{1,5},{5,1},{9,13},{13,9},{2,6},{6,2},{1... | collective-permute-start | bytes 49160 | tf_op jit(solution)/shard_map/ppermute | solution.py:548
  99.2 15.4 %all-to-all-start.4 = ((f32[64,16,128]{2,1,0:T(8,128)}), f32[64,16,128]{2,1,0:T(8,128)S(1)}, u32[]{:S(2)}, u32[]{:S(2)}) async-start(f32[64,16,128]{2,1,0:T(8,128)} %get-tuple-element.44), calls=%async_computation.4 | async-start | bytes 1048576 | tf_op jit(solution)/shard_map/all_to_all | solution.py:544
  103.8 9.2 %collective-permute-start.8 = (f32[32,32]{1,0:T(8,128)S(1)}, f32[32,32]{1,0:T(8,128)S(1)}, u32[]{:S(2)}, u32[]{:S(2)}) collective-permute-start(f32[32,32]{1,0:T(8,128)S(1)} %get-tuple-element.41.a_0_), channel_id=1, source_target_pairs={{0,3},{1,2},{2,1},{3,0},{4,7},{5,6},{6,5},{7,4},{8,11},{9,10},{10,... | collective-permute-start | bytes 12296 | tf_op jit(solution)/shard_map/ppermute | solution.py:548
  108.3 4.6 %collective-permute-start.7 = (f32[32,32]{1,0:T(8,128)S(1)}, f32[32,32]{1,0:T(8,128)S(1)}, u32[]{:S(2)}, u32[]{:S(2)}) collective-permute-start(f32[32,32]{1,0:T(8,128)S(1)} %get-tuple-element.41.a_0_), channel_id=1, source_target_pairs={{0,2},{1,3},{2,0},{3,1},{4,6},{5,7},{6,4},{7,5},{8,10},{9,11},{10,... | collective-permute-start | bytes 12296 | tf_op jit(solution)/shard_map/ppermute | solution.py:548
  108.5 4.5 %collective-permute-start.6 = (f32[32,32]{1,0:T(8,128)S(1)}, f32[32,32]{1,0:T(8,128)S(1)}, u32[]{:S(2)}, u32[]{:S(2)}) collective-permute-start(f32[32,32]{1,0:T(8,128)S(1)} %get-tuple-element.41.a_0_), channel_id=1, source_target_pairs={{0,1},{1,0},{2,3},{3,2},{4,5},{5,4},{6,7},{7,6},{8,9},{9,8},{10,11... | collective-permute-start | bytes 12296 | tf_op jit(solution)/shard_map/ppermute | solution.py:548
  114.6 5.5 %collective-permute-start.9 = (f32[16,128]{1,0:T(8,128)S(1)}, f32[16,128]{1,0:T(8,128)S(1)}, u32[]{:S(2)}, u32[]{:S(2)}) collective-permute-start(f32[16,128]{1,0:T(8,128)S(1)} %reduce_sum.19.own), channel_id=1, source_target_pairs={{0,1},{1,0},{2,3},{3,2},{4,5},{5,4},{6,7},{7,6},{8,9},{9,8},{10,11... | collective-permute-start | bytes 24584 | tf_op jit(solution)/shard_map/ppermute | solution.py:540
  135.7 2.8 %collective-permute-start.10 = (f32[64,8,128]{2,1,0:T(8,128)S(1)}, f32[64,8,128]{2,1,0:T(8,128)S(1)}, u32[]{:S(2)}, u32[]{:S(2)}) collective-permute-start(f32[64,8,128]{2,1,0:T(8,128)S(1)} %all_to_all.32.own), channel_id=1, source_target_pairs={{0,1},{1,0},{2,3},{3,2},{4,5},{5,4},{6,7},{7,6},{8,9},{9,8},{10,11... | collective-permute-start | bytes 786440 | tf_op jit(solution)/shard_map/ppermute | solution.py:540

commit v2 on v1

--- a/solution.py
+++ b/solution.py
@@ -244,8 +244,9 @@
     )(sketch)
 
 
-def second_kernel(scale, core_id, grams, z, sk, w, q, factor, mine, other, pair_w, sems):
+def project_kernel(z, w, u, pair_w, sems):
     r3 = pair_w.shape[0]
+    r1 = z.shape[0]
     each = r3 // sems.shape[0]
 
     def copy(i):
@@ -257,33 +258,63 @@
         return 0
 
     lax.fori_loop(0, r3 // each, start, 0)
-    g = unfold(tree_sum([grams[i] for i in range(grams.shape[0])]))
-    qv = dot(cholesky_inverse(g), z[...], 1, 0, HIGH)
-    q[...] = qv
-    factor[...] = qv * scale
-    hi, lo = split(qv)
-    v = dot(sk[...], jnp.concatenate([hi, hi, lo, lo], 0))
-    half = mine.shape[0]
-    k = 2 * half
-    acc = None
+    lhs = twice(z[...])
     for c in range(r3):
         if c % each == 0:
             copy(c // each).wait()
-        o = dot(twice(v[c * k : (c + 1) * k]), pair_w[c])
+        o = dot(lhs, pair_w[c])
+        hi, lo = split(o[r1:] + o[:r1])
+        u[c * r1 : (c + 1) * r1, :] = jnp.concatenate([hi, lo], 1)
+
+
+def project(z, w, r3):
+    r1, nx = z.shape
+    ny = w.shape[2]
+    return pl.pallas_call(
+        project_kernel,
+        in_specs=[VMEM, HBM],
+        out_specs=VMEM,
+        out_shape=jax.ShapeDtypeStruct((r3 * r1, 2 * ny), BF16),
+        scratch_shapes=[
+            pltpu.VMEM((r3, 2 * nx, ny), BF16),
+            pltpu.SemaphoreType.DMA((2,)),
+        ],
+        compiler_params=room(BIG),
+        cost_estimate=pl.CostEstimate(flops=10**9, bytes_accessed=6 * 10**6, transcendentals=0),
+    )(z, w)
+
+
+def second_kernel(scale, core_id, grams, z, sk, u, q, factor, mine, other):
+    g = unfold(tree_sum([grams[i] for i in range(grams.shape[0])]))
+    inv = cholesky_inverse(g)
+    hi, lo = split(inv)
+    mixed = dot(sk[...], jnp.concatenate([hi, hi, lo, lo], 0))
+    half = mine.shape[0]
+    k = 2 * half
+    ny = mine.shape[1]
+    r1 = z.shape[0]
+    group = 4
+    acc = None
+    for c in range(0, mixed.shape[0] // k, group):
+        left = jnp.concatenate([mixed[(c + i) * k : (c + i + 1) * k] for i in range(group)], 1)
+        hi, lo = split(left)
+        o = dot(jnp.concatenate([hi, lo], 0), u[c * r1 : (c + group) * r1, :])
         acc = o if acc is None else acc + o
-    zy = acc[k:] + acc[:k]
+    zy = (acc[k:, :ny] + acc[:k, ny:] + acc[k:, ny:]) + acc[:k, :ny]
     first = core_id[0] == 0
     mine[...] = jnp.where(first, zy[:half], zy[half:])
     other[...] = jnp.where(first, zy[half:], zy[:half])
-
-
-def second(core_id, grams, z, sk, w, scale, r3):
+    qv = dot(inv, z[...], 1, 0, HIGH)
+    q[...] = qv
+    factor[...] = qv * scale
+
+
+def second(core_id, grams, z, sk, u, scale, r3):
     r1, nx = z.shape
-    ny = w.shape[2]
-    half = jax.ShapeDtypeStruct((sk.shape[0] // r3 // 2, ny), F32)
+    half = jax.ShapeDtypeStruct((sk.shape[0] // r3 // 2, u.shape[1] // 2), F32)
     return pl.pallas_call(
         lambda *a: second_kernel(scale, *a),
-        in_specs=[SMEM, VMEM, VMEM, VMEM, HBM],
+        in_specs=[SMEM] + [VMEM] * 4,
         out_specs=[VMEM] * 4,
         out_shape=[
             jax.ShapeDtypeStruct((r1, nx), F32),
@@ -291,12 +322,8 @@
             half,
             half,
         ],
-        scratch_shapes=[
-            pltpu.VMEM((r3, 2 * nx, ny), BF16),
-            pltpu.SemaphoreType.DMA((4,)),
-        ],
-        compiler_params=room(BIG),
-    )(core_id, grams, z, sk, w)
+        compiler_params=room(8 * 1024 * 1024),
+    )(core_id, grams, z, sk, u)
 
 
 def contract_x_kernel(q, field, wx, held, out, lhs, sems, out_sems):
@@ -545,7 +572,8 @@
 
 
 def of_four(x, axes):
-    return [x] + [lax.ppermute(x, axes, [(i, i ^ s) for i in range(4)]) for s in (1, 2, 3)]
+    others = [lax.ppermute(x, axes, [(i, i ^ s) for i in range(4)]) for s in (3, 2, 1)]
+    return [x] + others[::-1]
 
 
 def spread(x, axes):
@@ -574,18 +602,19 @@
     zx = exchange(zx, ("z", "l"))
     zx, gx = gram_of(8, zx, pair(zx))
     sk_y = prepared_y(sketch_y.T, r3)
-    qx, factor_x, mine, other = second(
-        core_id, exchange(gx, ("y", "h")), zx, sk_y, w, scale_x, r3
-    )
+    u = project(zx, w, r3)
+    gx, u = lax.optimization_barrier((exchange(gx, ("y", "h")), u))
+    qx, factor_x, mine, other = second(core_id, gx, zx, sk_y, u, scale_x, r3)
     wx = contract_x(qx, field)
     zy = spread(mine + pair(other), ("y", "h", "l")).sum(0)
     zy, wx = lax.optimization_barrier((zy, wx))
     zy, gy = gram_of(1, both(zy, 0)[None])
     factor_y, part, zt = third(of_four(gy[0], "z"), zy, sketch_t.T, wx, scale_y, 32, r1)
     zt, gt, core = core_terms(exchange(zt, ("y", "h", "z")), part, r1)
-    factor_t, inv_t = last_factor(of_four(gt, ("l", "c")), zt, scale_t)
     chips = ("y", "h", "z", "l")
-    piece, inv_t = lax.optimization_barrier((exchange(core, chips).sum(0), inv_t))
+    piece = exchange(core, chips).sum(0)
+    piece, gt = lax.optimization_barrier((piece, of_four(gt, ("l", "c"))))
+    factor_t, inv_t = last_factor(gt, zt, scale_t)
     core = exchange(scaled(core_id, inv_t, piece, pair(piece), r1), chips)
     core = joined(core_id, core, pair(core))
     return factor_x.T, factor_y.T, factor_t.T, core

time: 140 us -> 140 us (level)
  waiting for transfers between devices: 16.6 us -> 14.6 us
  Pallas kernels: 39.9 us -> 41.7 us
    ppermute x6, waiting for transfers between devices: 5.79 us -> 1.84 us  [of_four(): lax.ppermute(x, axes, [(i, i ^ s) for i in range(4)])]
    all_to_all x3, waiting for transfers between devices: 5.92 us -> 8.75 us  [exchange(): return lax.all_to_all(x, axes, 0, 0)]
    pallas_call x1 -> x2, Pallas kernels: 4.5 us -> 6.29 us  [the longest x1 3.6 us: second(): pl.pallas_call(lambda *a: second_kernel(scale, *a), in_specs=[SMEM] + [VM...]
  transfers between devices with their start and end apart: 14 -> 14, of which waited for: 10 -> 8; matrix products, arithmetic and copies ran while one was open for 0% -> 0% of each run, Pallas kernels for 10% -> 12%
where the time goes in v2:
time: 140 us; the launch traced here: 139 us
  blocking collectives  46.2 us (33%)
  Pallas kernels  41.7 us (30%)
  starting transfers between devices  34.8 us (25%)
  waiting for transfers between devices  14.6 us (10%)
    all_to_all x3, blocking collectives, exchange(): return lax.all_to_all(x, axes, 0, 0)  46.2 us
    all_to_all x3, starting transfers between devices, exchange(): return lax.all_to_all(x, axes, 0, 0)  14.6 us
    pallas_call x1, Pallas kernels, first(): pl.pallas_call(first_kernel, in_specs=[HBM, HBM, HBM, HBM], out_specs=[HB...  11.9 us
    pallas_call x1, Pallas kernels, contract_x(): pl.pallas_call(contract_x_kernel, in_specs=[VMEM, HBM], out_specs=HBM, ou...  11.5 us
    ppermute x5, starting transfers between devices, pair(): return lax.ppermute(x, 'c', [(0, 1), (1, 0)])  11.2 us
    ppermute x6, starting transfers between devices, of_four(): lax.ppermute(x, axes, [(i, i ^ s) for i in range(4)])  9.05 us
    all_to_all x3, waiting for transfers between devices, exchange(): return lax.all_to_all(x, axes, 0, 0)  8.75 us
    pallas_call x1, Pallas kernels, third(): pl.pallas_call(lambda *a: third_kernel(scale, *a), in_specs=[VMEM] * 6 +...  5.06 us
  transfers between devices with their start and end apart: 14, of which 8 were waited for; matrix products, arithmetic and copies ran while one was open for 0% of the time, Pallas kernels for 12%

profile of v2, /device:TPU:1, one launch (start us, length us, event | category | flops | bytes accessed | tf_op | source)
XLA Modules:
  0.0 139.1 jit_solution(6900591831367422135)
XLA Ops:
  0.6 0.0 copy-start
  0.6 11.9 %shard_map.93 = (bf16[128,256,256]{2,1,0:T(8,128)(2,1)}, f32[8,64,128]{2,1,0:T(8,128)}) custom-call(f32[128,256,128]{2,1,0:T(8,128)} %field.3, f32[32,128]{1,0:T(8,128)} %bitcast.22, f32[64,256]{1,0:T(8,128)} %bitcast.20, f32[64,2048]{1,0:T(8,128)} %bitcast.18), custom_call_target="tpu_custom_call" | custom-call | flops 1073741824 | bytes 16777216 | tf_op jit(solution)/shard_map/pallas_call | solution.py:174
  12.6 13.0 %all_to_all.30.refs_0_ = f32[8,64,128]{2,1,0:T(8,128)S(1)} all-to-all(f32[8,64,128]{2,1,0:T(8,128)} %get-tuple-element.31), channel_id=1, replica_groups=mesh['y'=4,'h'=2,'z'=4,'l'=2,'c'=2] {'z','l'}, dimensions={0} | all-to-all | bytes 524288 | tf_op jit(solution)/shard_map/all_to_all | solution.py:571
  25.6 2.1 %collective-permute-start = (f32[8,64,128]{2,1,0:T(8,128)S(1)}, f32[8,64,128]{2,1,0:T(8,128)S(1)}, u32[]{:S(2)}, u32[]{:S(2)}) collective-permute-start(f32[8,64,128]{2,1,0:T(8,128)S(1)} %all_to_all.30.refs_0_), channel_id=1, source_target_pairs={{0,1},{1,0},{2,3},{3,2},{4,5},{5,4},{6,7},{7,6},{8,9},{9,8},{10,11... | collective-permute-start | bytes 786440 | tf_op jit(solution)/shard_map/ppermute | solution.py:567
  27.6 1.2 collective-permute-done.refs_1_
  28.8 0.9 shard_map.94
  29.7 6.4 %all-to-all-start.1 = ((f32[8,32,128]{2,1,0:T(8,128)}), f32[8,32,128]{2,1,0:T(8,128)S(1)}, u32[]{:S(2)}, u32[]{:S(2)}) async-start(f32[8,32,128]{2,1,0:T(8,128)} %get-tuple-element.32), calls=%async_computation.1 | async-start | bytes 262144 | tf_op jit(solution)/shard_map/all_to_all | solution.py:571
  36.1 0.0 copy-done
  36.1 1.1 shard_map.96.a_3_
  37.2 2.7 %shard_map.95.a_4_ = bf16[2048,512]{1,0:T(8,128)(2,1)S(1)} custom-call(f32[64,128]{1,0:T(8,128)S(1)} %get-tuple-element.33.z.a_2_, bf16[128,256,256]{2,1,0:T(8,128)(2,1)} %get-tuple-element.34.w), custom_call_target="tpu_custom_call" | custom-call | flops 1000000000 | bytes 6000000 | tf_op jit(solution)/shard_map/pallas_call | solution.py:273
  39.9 3.2 %all-to-all-done.1.a_1_ = f32[8,32,128]{2,1,0:T(8,128)S(1)} async-done(((f32[8,32,128]{2,1,0:T(8,128)}), f32[8,32,128]{2,1,0:T(8,128)S(1)}, u32[]{:S(2)}, u32[]{:S(2)}) %all-to-all-start.1) | async-done | bytes 131104 | tf_op jit(solution)/shard_map/all_to_all | solution.py:571
  43.1 3.6 %shard_map.97 = (f32[64,128]{1,0:T(8,128)S(1)}, f32[64,128]{1,0:T(8,128)}, f32[32,256]{1,0:T(8,128)S(1)}, f32[32,256]{1,0:T(8,128)S(1)}) custom-call(s32[1]{0:T(128)} %bitcast.a_0_.core_id, f32[8,32,128]{2,1,0:T(8,128)S(1)} %all-to-all-done.1.a_1_, f32[64,128]{1,0:T(8,128)S(1)} %get-tuple-element.33.z.a_2_, bf16[2048,256]{1,0:T(8,128)(2,1)S(1)} %shard_map.96.a_3_, ...), custom_call_target="tpu_custom_call" | custom-call | tf_op jit(solution)/shard_map/pallas_call | solution.py:315
  46.7 1.8 %collective-permute-start.1 = (f32[32,256]{1,0:T(8,128)S(1)}, f32[32,256]{1,0:T(8,128)S(1)}, u32[]{:S(2)}, u32[]{:S(2)}) collective-permute-start(f32[32,256]{1,0:T(8,128)S(1)} %get-tuple-element.39), channel_id=1, source_target_pairs={{0,1},{1,0},{2,3},{3,2},{4,5},{5,4},{6,7},{7,6},{8,9},{9,8},{10,11... | collective-permute-start | bytes 98312 | tf_op jit(solution)/shard_map/ppermute | solution.py:567
  48.5 0.9 collective-permute-done.1
  49.4 0.8 broadcast_in_dim.4
  50.2 3.6 %all-to-all-start.2 = ((f32[16,32,256]{2,1,0:T(8,128)}), f32[16,32,256]{2,1,0:T(8,128)S(1)}, u32[]{:S(2)}, u32[]{:S(2)}) async-start(f32[16,32,256]{2,1,0:T(8,128)} %broadcast_in_dim.4), calls=%async_computation.2 | async-start | bytes 1048576 | tf_op jit(solution)/shard_map/all_to_all | solution.py:571
  53.8 0.0 copy-start.1
  53.8 11.5 %shard_map.98.a_6_ = f32[128,256,128]{2,1,0:T(8,128)} custom-call(f32[64,128]{1,0:T(8,128)S(1)} %get-tuple-element.40.q, f32[128,256,128]{2,1,0:T(8,128)} %field.3), custom_call_target="tpu_custom_call" | custom-call | flops 2147483648 | bytes 25165824 | tf_op jit(solution)/shard_map/pallas_call | solution.py:382
  65.4 0.0 all-to-all-done.2
  65.4 1.0 collective-permute-start.2
  66.4 0.9 collective-permute-done.2
  67.3 0.3 shard_map.99
  67.5 0.3 collective-permute-start.3
  67.8 1.6 %collective-permute-start.4 = (f32[32,128]{1,0:T(8,128)S(1)}, f32[32,128]{1,0:T(8,128)S(1)}, u32[]{:S(2)}, u32[]{:S(2)}) collective-permute-start(f32[32,128]{1,0:T(8,128)S(1)} %bitcast.15), channel_id=1, source_target_pairs={{0,8},{4,12},{8,0},{12,4},{1,9},{5,13},{9,1},{13,5},{2,10},{6,14},... | collective-permute-start | bytes 49160 | tf_op jit(solution)/shard_map/ppermute | solution.py:575
  69.4 2.0 %collective-permute-start.5 = (f32[32,128]{1,0:T(8,128)S(1)}, f32[32,128]{1,0:T(8,128)S(1)}, u32[]{:S(2)}, u32[]{:S(2)}) collective-permute-start(f32[32,128]{1,0:T(8,128)S(1)} %bitcast.16), channel_id=1, source_target_pairs={{0,12},{4,8},{8,4},{12,0},{1,13},{5,9},{9,5},{13,1},{2,14},{6,10},... | collective-permute-start | bytes 49160 | tf_op jit(solution)/shard_map/ppermute | solution.py:575
  71.4 0.0 collective-permute-done.3.a_1_
  71.4 0.4 collective-permute-done.4.a_2_
  71.9 1.4 collective-permute-done.5.a_3_
  73.2 0.0 copy-done.1
  73.2 5.1 %shard_map.100 = (f32[64,256]{1,0:T(8,128)}, bf16[4096,256]{1,0:T(8,128)(2,1)S(1)}, f32[32,32,128]{2,1,0:T(8,128)S(1)}) custom-call(f32[32,128]{1,0:T(8,128)S(1)} %bitcast.17, f32[32,128]{1,0:T(8,128)S(1)} %collective-permute-done.3.a_1_, f32[32,128]{1,0:T(8,128)S(1)} %collective-permute-done.4.a_2_, f32[32,128]{1,0:T(8,128)S(1)} %collective-permute-done.5.a_3_, ...), custom_call_target="tpu_custom_call" | custom-call | tf_op jit(solution)/shard_map/pallas_call | solution.py:452
  78.3 18.9 %all_to_all.31.parts = f32[32,32,128]{2,1,0:T(8,128)S(1)} all-to-all(f32[32,32,128]{2,1,0:T(8,128)S(1)} %get-tuple-element.46), channel_id=1, replica_groups=mesh['y'=4,'h'=2,'z'=4,'l'=2,'c'=2] {'y','h','z'}, dimensions={0} | all-to-all | bytes 1048576 | tf_op jit(solution)/shard_map/all_to_all | solution.py:571
  97.2 1.7 %shard_map.101 = (f32[32,128]{1,0:T(8,128)S(1)}, f32[32,32]{1,0:T(8,128)S(1)}, f32[64,16,128]{2,1,0:T(8,128)}) custom-call(f32[32,32,128]{2,1,0:T(8,128)S(1)} %all_to_all.31.parts, bf16[4096,256]{1,0:T(8,128)(2,1)S(1)} %get-tuple-element.47.part), custom_call_target="tpu_custom_call" | custom-call | tf_op jit(solution)/shard_map/pallas_call | solution.py:490
  99.0 4.6 %all-to-all-start.4 = ((f32[64,16,128]{2,1,0:T(8,128)}), f32[64,16,128]{2,1,0:T(8,128)S(1)}, u32[]{:S(2)}, u32[]{:S(2)}) async-start(f32[64,16,128]{2,1,0:T(8,128)} %get-tuple-element.48), calls=%async_computation.4 | async-start | bytes 1048576 | tf_op jit(solution)/shard_map/all_to_all | solution.py:571
  103.6 3.4 %collective-permute-start.6 = (f32[32,32]{1,0:T(8,128)S(1)}, f32[32,32]{1,0:T(8,128)S(1)}, u32[]{:S(2)}, u32[]{:S(2)}) collective-permute-start(f32[32,32]{1,0:T(8,128)S(1)} %get-tuple-element.50.a_0_), channel_id=1, source_target_pairs={{0,1},{1,0},{2,3},{3,2},{4,5},{5,4},{6,7},{7,6},{8,9},{9,8},{10,11... | collective-permute-start | bytes 12296 | tf_op jit(solution)/shard_map/ppermute | solution.py:575
  107.0 1.3 collective-permute-start.7
  108.4 0.4 collective-permute-start.8
  108.8 5.5 %all-to-all-done.4 = f32[64,16,128]{2,1,0:T(8,128)S(1)} async-done(((f32[64,16,128]{2,1,0:T(8,128)}), f32[64,16,128]{2,1,0:T(8,128)S(1)}, u32[]{:S(2)}, u32[]{:S(2)}) %all-to-all-start.4) | async-done | bytes 524320 | tf_op jit(solution)/shard_map/all_to_all | solution.py:571
  114.3 0.1 reduce_sum.19.own
  114.4 0.0 collective-permute-done.6.a_1_
  114.4 0.0 collective-permute-done.7.a_2_
  114.4 0.0 collective-permute-done.8.a_3_
  114.4 4.8 %collective-permute-start.9 = (f32[16,128]{1,0:T(8,128)S(1)}, f32[16,128]{1,0:T(8,128)S(1)}, u32[]{:S(2)}, u32[]{:S(2)}) collective-permute-start(f32[16,128]{1,0:T(8,128)S(1)} %reduce_sum.19.own), channel_id=1, source_target_pairs={{0,1},{1,0},{2,3},{3,2},{4,5},{5,4},{6,7},{7,6},{8,9},{9,8},{10,11... | collective-permute-start | bytes 24584 | tf_op jit(solution)/shard_map/ppermute | solution.py:567
  119.2 1.6 %shard_map.102 = (f32[32,128]{1,0:T(8,128)}, f32[32,32]{1,0:T(8,128)S(1)}) custom-call(f32[32,32]{1,0:T(8,128)S(1)} %get-tuple-element.50.a_0_, f32[32,32]{1,0:T(8,128)S(1)} %collective-permute-done.6.a_1_, f32[32,32]{1,0:T(8,128)S(1)} %collective-permute-done.7.a_2_, f32[32,32]{1,0:T(8,128)S(1)} %collective-permute-done.8.a_3_, ...), custom_call_target="tpu_custom_call" | custom-call | flops 10000000 | bytes 2000000 | tf_op jit(solution)/shard_map/pallas_call | solution.py:510
  120.8 0.0 collective-permute-done.9.other
  120.8 0.4 shard_map.103
  121.2 14.3 %all_to_all.32.own = f32[64,8,128]{2,1,0:T(8,128)S(1)} all-to-all(f32[64,8,128]{2,1,0:T(8,128)S(1)} %shard_map.103), channel_id=1, replica_groups=mesh['y'=4,'h'=2,'z'=4,'l'=2,'c'=2] {'y','h','z','l'}, dimensions={0} | all-to-all | bytes 524288 | tf_op jit(solution)/shard_map/all_to_all | solution.py:571
  135.5 1.5 %collective-permute-start.10 = (f32[64,8,128]{2,1,0:T(8,128)S(1)}, f32[64,8,128]{2,1,0:T(8,128)S(1)}, u32[]{:S(2)}, u32[]{:S(2)}) collective-permute-start(f32[64,8,128]{2,1,0:T(8,128)S(1)} %all_to_all.32.own), channel_id=1, source_target_pairs={{0,1},{1,0},{2,3},{3,2},{4,5},{5,4},{6,7},{7,6},{8,9},{9,8},{10,11... | collective-permute-start | bytes 786440 | tf_op jit(solution)/shard_map/ppermute | solution.py:567
  137.0 1.2 collective-permute-done.10.other
  138.2 0.9 shard_map.104
  (3 shorter events, 0.0 us)
Async XLA Ops:
  0.6 35.4 %copy-start = (f32[2048,64]{0,1:T(8,128)S(1)}, f32[2048,64]{0,1:T(8,128)}, u32[]{:S(2)}) copy-start(f32[2048,64]{0,1:T(8,128)} %param.10) | copy-start | bytes 1572868
  25.6 3.2 %collective-permute-start = (f32[8,64,128]{2,1,0:T(8,128)S(1)}, f32[8,64,128]{2,1,0:T(8,128)S(1)}, u32[]{:S(2)}, u32[]{:S(2)}) collective-permute-start(f32[8,64,128]{2,1,0:T(8,128)S(1)} %all_to_all.30.refs_0_), channel_id=1, source_target_pairs={{0,1},{1,0},{2,3},{3,2},{4,5},{5,4},{6,7},{7,6},{8,9},{9,8},{10,11... | collective-permute-start | bytes 786440 | tf_op jit(solution)/shard_map/ppermute | solution.py:567
  29.7 13.4 %all-to-all-start.1 = ((f32[8,32,128]{2,1,0:T(8,128)}), f32[8,32,128]{2,1,0:T(8,128)S(1)}, u32[]{:S(2)}, u32[]{:S(2)}) async-start(f32[8,32,128]{2,1,0:T(8,128)} %get-tuple-element.32), calls=%async_computation.1 | async-start | bytes 262144 | tf_op jit(solution)/shard_map/all_to_all | solution.py:571
  46.7 2.7 %collective-permute-start.1 = (f32[32,256]{1,0:T(8,128)S(1)}, f32[32,256]{1,0:T(8,128)S(1)}, u32[]{:S(2)}, u32[]{:S(2)}) collective-permute-start(f32[32,256]{1,0:T(8,128)S(1)} %get-tuple-element.39), channel_id=1, source_target_pairs={{0,1},{1,0},{2,3},{3,2},{4,5},{5,4},{6,7},{7,6},{8,9},{9,8},{10,11... | collective-permute-start | bytes 98312 | tf_op jit(solution)/shard_map/ppermute | solution.py:567
  50.2 15.1 %all-to-all-start.2 = ((f32[16,32,256]{2,1,0:T(8,128)}), f32[16,32,256]{2,1,0:T(8,128)S(1)}, u32[]{:S(2)}, u32[]{:S(2)}) async-start(f32[16,32,256]{2,1,0:T(8,128)} %broadcast_in_dim.4), calls=%async_computation.2 | async-start | bytes 1048576 | tf_op jit(solution)/shard_map/all_to_all | solution.py:571
  53.8 19.4 %copy-start.1 = (f32[4096,32]{0,1:T(8,128)S(1)}, f32[4096,32]{0,1:T(8,128)}, u32[]{:S(2)}) copy-start(f32[4096,32]{0,1:T(8,128)} %param.11) | copy-start | bytes 1572868
  65.4 1.8 %collective-permute-start.2 = (f32[32,256]{1,0:T(8,128)S(1)}, f32[32,256]{1,0:T(8,128)S(1)}, u32[]{:S(2)}, u32[]{:S(2)}) collective-permute-start(f32[32,256]{1,0:T(8,128)S(1)} %reduce_sum.18), channel_id=1, source_target_pairs={{0,1},{1,0},{2,3},{3,2},{4,5},{5,4},{6,7},{7,6},{8,9},{9,8},{10,11... | collective-permute-start | bytes 98312 | tf_op jit(solution)/shard_map/ppermute | solution.py:567
  67.5 3.9 %collective-permute-start.3 = (f32[32,128]{1,0:T(8,128)S(1)}, f32[32,128]{1,0:T(8,128)S(1)}, u32[]{:S(2)}, u32[]{:S(2)}) collective-permute-start(f32[32,128]{1,0:T(8,128)S(1)} %bitcast.14), channel_id=1, source_target_pairs={{0,4},{4,0},{8,12},{12,8},{1,5},{5,1},{9,13},{13,9},{2,6},{6,2},{1... | collective-permute-start | bytes 49160 | tf_op jit(solution)/shard_map/ppermute | solution.py:575
  67.8 4.1 %collective-permute-start.4 = (f32[32,128]{1,0:T(8,128)S(1)}, f32[32,128]{1,0:T(8,128)S(1)}, u32[]{:S(2)}, u32[]{:S(2)}) collective-permute-start(f32[32,128]{1,0:T(8,128)S(1)} %bitcast.15), channel_id=1, source_target_pairs={{0,8},{4,12},{8,0},{12,4},{1,9},{5,13},{9,1},{13,5},{2,10},{6,14},... | collective-permute-start | bytes 49160 | tf_op jit(solution)/shard_map/ppermute | solution.py:575
  69.4 3.9 %collective-permute-start.5 = (f32[32,128]{1,0:T(8,128)S(1)}, f32[32,128]{1,0:T(8,128)S(1)}, u32[]{:S(2)}, u32[]{:S(2)}) collective-permute-start(f32[32,128]{1,0:T(8,128)S(1)} %bitcast.16), channel_id=1, source_target_pairs={{0,12},{4,8},{8,4},{12,0},{1,13},{5,9},{9,5},{13,1},{2,14},{6,10},... | collective-permute-start | bytes 49160 | tf_op jit(solution)/shard_map/ppermute | solution.py:575
  99.0 15.3 %all-to-all-start.4 = ((f32[64,16,128]{2,1,0:T(8,128)}), f32[64,16,128]{2,1,0:T(8,128)S(1)}, u32[]{:S(2)}, u32[]{:S(2)}) async-start(f32[64,16,128]{2,1,0:T(8,128)} %get-tuple-element.48), calls=%async_computation.4 | async-start | bytes 1048576 | tf_op jit(solution)/shard_map/all_to_all | solution.py:571
  103.6 10.8 %collective-permute-start.6 = (f32[32,32]{1,0:T(8,128)S(1)}, f32[32,32]{1,0:T(8,128)S(1)}, u32[]{:S(2)}, u32[]{:S(2)}) collective-permute-start(f32[32,32]{1,0:T(8,128)S(1)} %get-tuple-element.50.a_0_), channel_id=1, source_target_pairs={{0,1},{1,0},{2,3},{3,2},{4,5},{5,4},{6,7},{7,6},{8,9},{9,8},{10,11... | collective-permute-start | bytes 12296 | tf_op jit(solution)/shard_map/ppermute | solution.py:575
  107.0 7.3 %collective-permute-start.7 = (f32[32,32]{1,0:T(8,128)S(1)}, f32[32,32]{1,0:T(8,128)S(1)}, u32[]{:S(2)}, u32[]{:S(2)}) collective-permute-start(f32[32,32]{1,0:T(8,128)S(1)} %get-tuple-element.50.a_0_), channel_id=1, source_target_pairs={{0,2},{1,3},{2,0},{3,1},{4,6},{5,7},{6,4},{7,5},{8,10},{9,11},{10,... | collective-permute-start | bytes 12296 | tf_op jit(solution)/shard_map/ppermute | solution.py:575
  108.4 6.1 %collective-permute-start.8 = (f32[32,32]{1,0:T(8,128)S(1)}, f32[32,32]{1,0:T(8,128)S(1)}, u32[]{:S(2)}, u32[]{:S(2)}) collective-permute-start(f32[32,32]{1,0:T(8,128)S(1)} %get-tuple-element.50.a_0_), channel_id=1, source_target_pairs={{0,3},{1,2},{2,1},{3,0},{4,7},{5,6},{6,5},{7,4},{8,11},{9,10},{10,... | collective-permute-start | bytes 12296 | tf_op jit(solution)/shard_map/ppermute | solution.py:575
  114.4 6.4 %collective-permute-start.9 = (f32[16,128]{1,0:T(8,128)S(1)}, f32[16,128]{1,0:T(8,128)S(1)}, u32[]{:S(2)}, u32[]{:S(2)}) collective-permute-start(f32[16,128]{1,0:T(8,128)S(1)} %reduce_sum.19.own), channel_id=1, source_target_pairs={{0,1},{1,0},{2,3},{3,2},{4,5},{5,4},{6,7},{7,6},{8,9},{9,8},{10,11... | collective-permute-start | bytes 24584 | tf_op jit(solution)/shard_map/ppermute | solution.py:567
  135.5 2.7 %collective-permute-start.10 = (f32[64,8,128]{2,1,0:T(8,128)S(1)}, f32[64,8,128]{2,1,0:T(8,128)S(1)}, u32[]{:S(2)}, u32[]{:S(2)}) collective-permute-start(f32[64,8,128]{2,1,0:T(8,128)S(1)} %all_to_all.32.own), channel_id=1, source_target_pairs={{0,1},{1,0},{2,3},{3,2},{4,5},{5,4},{6,7},{7,6},{8,9},{9,8},{10,11... | collective-permute-start | bytes 786440 | tf_op jit(solution)/shard_map/ppermute | solution.py:567

commit v3 on v2

--- a/solution.py
+++ b/solution.py
@@ -599,8 +599,8 @@
     core_id = lax.axis_index("c").astype(jnp.int32).reshape(1)
 
     w, zx = first(field, init_t.T, init_y.T, sketch_x.T, 8)
-    zx = exchange(zx, ("z", "l"))
-    zx, gx = gram_of(8, zx, pair(zx))
+    zx = exchange(zx, ("z", "l")).sum(0)
+    zx, gx = gram_of(8, zx[None], pair(zx)[None])
     sk_y = prepared_y(sketch_y.T, r3)
     u = project(zx, w, r3)
     gx, u = lax.optimization_barrier((exchange(gx, ("y", "h")), u))
@@ -613,8 +613,8 @@
     zt, gt, core = core_terms(exchange(zt, ("y", "h", "z")), part, r1)
     chips = ("y", "h", "z", "l")
     piece = exchange(core, chips).sum(0)
-    piece, gt = lax.optimization_barrier((piece, of_four(gt, ("l", "c"))))
-    factor_t, inv_t = last_factor(gt, zt, scale_t)
+    factor_t, inv_t = last_factor(of_four(gt, ("l", "c")), zt, scale_t)
+    piece, inv_t = lax.optimization_barrier((piece, inv_t))
     core = exchange(scaled(core_id, inv_t, piece, pair(piece), r1), chips)
     core = joined(core_id, core, pair(core))
     return factor_x.T, factor_y.T, factor_t.T, core

time: 140 us -> 139 us (level)
    all_to_all x3, waiting for transfers between devices: 8.75 us -> 3.22 us  [exchange(): return lax.all_to_all(x, axes, 0, 0)]
    ppermute x6, waiting for transfers between devices: 1.84 us -> 6.1 us  [of_four(): lax.ppermute(x, axes, [(i, i ^ s) for i in range(4)])]
  transfers between devices with their start and end apart: 14 -> 14, of which waited for: 8 -> 10; matrix products, arithmetic and copies ran while one was open for 0% -> 0% of each run, Pallas kernels for 12% -> 12%
where the time goes in v3:
time: 139 us
  blocking collectives  46.8 us (34%)
  Pallas kernels  41.7 us (30%)
  starting transfers between devices  34.6 us (25%)
  waiting for transfers between devices  13.9 us (10%)
    all_to_all x3, blocking collectives, exchange(): return lax.all_to_all(x, axes, 0, 0)  46.8 us
    all_to_all x3, starting transfers between devices, exchange(): return lax.all_to_all(x, axes, 0, 0)  14.6 us
    pallas_call x1, Pallas kernels, first(): pl.pallas_call(first_kernel, in_specs=[HBM, HBM, HBM, HBM], out_specs=[HB...  11.9 us
    pallas_call x1, Pallas kernels, contract_x(): pl.pallas_call(contract_x_kernel, in_specs=[VMEM, HBM], out_specs=HBM, ou...  11.6 us
    ppermute x5, starting transfers between devices, pair(): return lax.ppermute(x, 'c', [(0, 1), (1, 0)])  11 us
    ppermute x6, starting transfers between devices, of_four(): lax.ppermute(x, axes, [(i, i ^ s) for i in range(4)])  9.05 us
    ppermute x6, waiting for transfers between devices, of_four(): lax.ppermute(x, axes, [(i, i ^ s) for i in range(4)])  6.1 us
    pallas_call x1, Pallas kernels, third(): pl.pallas_call(lambda *a: third_kernel(scale, *a), in_specs=[VMEM] * 6 +...  5.06 us
  transfers between devices with their start and end apart: 14, of which 10 were waited for; matrix products, arithmetic and copies ran while one was open for 0% of the time, Pallas kernels for 12%

profile of v3, /device:TPU:1, one launch (start us, length us, event | category | flops | bytes accessed | tf_op | source)
XLA Modules:
  0.0 138.7 jit_solution(6796866432601123068)
XLA Ops:
  0.6 0.0 copy-start
  0.6 11.9 %shard_map.93 = (bf16[128,256,256]{2,1,0:T(8,128)(2,1)}, f32[8,64,128]{2,1,0:T(8,128)}) custom-call(f32[128,256,128]{2,1,0:T(8,128)} %field.3, f32[32,128]{1,0:T(8,128)} %bitcast.26, f32[64,256]{1,0:T(8,128)} %bitcast.24, f32[64,2048]{1,0:T(8,128)} %bitcast.22), custom_call_target="tpu_custom_call" | custom-call | flops 1073741824 | bytes 16777216 | tf_op jit(solution)/shard_map/pallas_call | solution.py:174
  12.6 13.0 %all_to_all.30 = f32[8,64,128]{2,1,0:T(8,128)S(1)} all-to-all(f32[8,64,128]{2,1,0:T(8,128)} %get-tuple-element.28), channel_id=1, replica_groups=mesh['y'=4,'h'=2,'z'=4,'l'=2,'c'=2] {'z','l'}, dimensions={0} | all-to-all | bytes 524288 | tf_op jit(solution)/shard_map/all_to_all | solution.py:571
  25.6 2.1 %collective-permute-start = (f32[64,128]{1,0:T(8,128)S(1)}, f32[64,128]{1,0:T(8,128)S(1)}, u32[]{:S(2)}, u32[]{:S(2)}) collective-permute-start(f32[64,128]{1,0:T(8,128)S(1)} %reduce_sum.27), channel_id=1, source_target_pairs={{0,1},{1,0},{2,3},{3,2},{4,5},{5,4},{6,7},{7,6},{8,9},{9,8},{10,11... | collective-permute-start | bytes 98312 | tf_op jit(solution)/shard_map/ppermute | solution.py:567
  27.7 0.9 collective-permute-done
  28.6 0.9 shard_map.94
  29.5 6.4 %all-to-all-start.1 = ((f32[8,32,128]{2,1,0:T(8,128)}), f32[8,32,128]{2,1,0:T(8,128)S(1)}, u32[]{:S(2)}, u32[]{:S(2)}) async-start(f32[8,32,128]{2,1,0:T(8,128)} %get-tuple-element.29), calls=%async_computation.1 | async-start | bytes 262144 | tf_op jit(solution)/shard_map/all_to_all | solution.py:571
  35.9 0.0 copy-done
  35.9 1.1 shard_map.96.a_3_
  37.0 2.7 %shard_map.95.a_4_ = bf16[2048,512]{1,0:T(8,128)(2,1)S(1)} custom-call(f32[64,128]{1,0:T(8,128)S(1)} %get-tuple-element.30.z.a_2_, bf16[128,256,256]{2,1,0:T(8,128)(2,1)} %get-tuple-element.31.w), custom_call_target="tpu_custom_call" | custom-call | flops 1000000000 | bytes 6000000 | tf_op jit(solution)/shard_map/pallas_call | solution.py:273
  39.7 3.2 %all-to-all-done.1.a_1_ = f32[8,32,128]{2,1,0:T(8,128)S(1)} async-done(((f32[8,32,128]{2,1,0:T(8,128)}), f32[8,32,128]{2,1,0:T(8,128)S(1)}, u32[]{:S(2)}, u32[]{:S(2)}) %all-to-all-start.1) | async-done | bytes 131104 | tf_op jit(solution)/shard_map/all_to_all | solution.py:571
  42.9 3.6 %shard_map.97 = (f32[64,128]{1,0:T(8,128)S(1)}, f32[64,128]{1,0:T(8,128)}, f32[32,256]{1,0:T(8,128)S(1)}, f32[32,256]{1,0:T(8,128)S(1)}) custom-call(s32[1]{0:T(128)} %bitcast.a_0_.core_id, f32[8,32,128]{2,1,0:T(8,128)S(1)} %all-to-all-done.1.a_1_, f32[64,128]{1,0:T(8,128)S(1)} %get-tuple-element.30.z.a_2_, bf16[2048,256]{1,0:T(8,128)(2,1)S(1)} %shard_map.96.a_3_, ...), custom_call_target="tpu_custom_call" | custom-call | tf_op jit(solution)/shard_map/pallas_call | solution.py:315
  46.5 1.8 %collective-permute-start.1 = (f32[32,256]{1,0:T(8,128)S(1)}, f32[32,256]{1,0:T(8,128)S(1)}, u32[]{:S(2)}, u32[]{:S(2)}) collective-permute-start(f32[32,256]{1,0:T(8,128)S(1)} %get-tuple-element.36), channel_id=1, source_target_pairs={{0,1},{1,0},{2,3},{3,2},{4,5},{5,4},{6,7},{7,6},{8,9},{9,8},{10,11... | collective-permute-start | bytes 98312 | tf_op jit(solution)/shard_map/ppermute | solution.py:567
  48.3 0.9 collective-permute-done.1
  49.2 0.8 broadcast_in_dim.12
  50.0 3.6 %all-to-all-start.2 = ((f32[16,32,256]{2,1,0:T(8,128)}), f32[16,32,256]{2,1,0:T(8,128)S(1)}, u32[]{:S(2)}, u32[]{:S(2)}) async-start(f32[16,32,256]{2,1,0:T(8,128)} %broadcast_in_dim.12), calls=%async_computation.2 | async-start | bytes 1048576 | tf_op jit(solution)/shard_map/all_to_all | solution.py:571
  53.6 0.0 copy-start.1
  53.6 11.6 %shard_map.98.a_6_ = f32[128,256,128]{2,1,0:T(8,128)} custom-call(f32[64,128]{1,0:T(8,128)S(1)} %get-tuple-element.37.q, f32[128,256,128]{2,1,0:T(8,128)} %field.3), custom_call_target="tpu_custom_call" | custom-call | flops 2147483648 | bytes 25165824 | tf_op jit(solution)/shard_map/pallas_call | solution.py:382
  65.2 0.0 all-to-all-done.2
  65.2 0.9 collective-permute-start.2
  66.1 0.9 collective-permute-done.2
  67.0 0.3 shard_map.99
  67.3 0.3 collective-permute-start.3
  67.5 1.6 %collective-permute-start.4 = (f32[32,128]{1,0:T(8,128)S(1)}, f32[32,128]{1,0:T(8,128)S(1)}, u32[]{:S(2)}, u32[]{:S(2)}) collective-permute-start(f32[32,128]{1,0:T(8,128)S(1)} %bitcast.19), channel_id=1, source_target_pairs={{0,8},{4,12},{8,0},{12,4},{1,9},{5,13},{9,1},{13,5},{2,10},{6,14},... | collective-permute-start | bytes 49160 | tf_op jit(solution)/shard_map/ppermute | solution.py:575
  69.1 2.0 %collective-permute-start.5 = (f32[32,128]{1,0:T(8,128)S(1)}, f32[32,128]{1,0:T(8,128)S(1)}, u32[]{:S(2)}, u32[]{:S(2)}) collective-permute-start(f32[32,128]{1,0:T(8,128)S(1)} %bitcast.20), channel_id=1, source_target_pairs={{0,12},{4,8},{8,4},{12,0},{1,13},{5,9},{9,5},{13,1},{2,14},{6,10},... | collective-permute-start | bytes 49160 | tf_op jit(solution)/shard_map/ppermute | solution.py:575
  71.2 0.0 collective-permute-done.3.a_1_
  71.2 0.4 collective-permute-done.4.a_2_
  71.6 1.4 collective-permute-done.5.a_3_
  73.0 0.0 copy-done.1
  73.0 5.1 %shard_map.100 = (f32[64,256]{1,0:T(8,128)}, bf16[4096,256]{1,0:T(8,128)(2,1)S(1)}, f32[32,32,128]{2,1,0:T(8,128)S(1)}) custom-call(f32[32,128]{1,0:T(8,128)S(1)} %bitcast.21, f32[32,128]{1,0:T(8,128)S(1)} %collective-permute-done.3.a_1_, f32[32,128]{1,0:T(8,128)S(1)} %collective-permute-done.4.a_2_, f32[32,128]{1,0:T(8,128)S(1)} %collective-permute-done.5.a_3_, ...), custom_call_target="tpu_custom_call" | custom-call | tf_op jit(solution)/shard_map/pallas_call | solution.py:452
  78.1 18.8 %all_to_all.31.parts = f32[32,32,128]{2,1,0:T(8,128)S(1)} all-to-all(f32[32,32,128]{2,1,0:T(8,128)S(1)} %get-tuple-element.43), channel_id=1, replica_groups=mesh['y'=4,'h'=2,'z'=4,'l'=2,'c'=2] {'y','h','z'}, dimensions={0} | all-to-all | bytes 1048576 | tf_op jit(solution)/shard_map/all_to_all | solution.py:571
  96.9 1.7 %shard_map.101 = (f32[32,128]{1,0:T(8,128)S(1)}, f32[32,32]{1,0:T(8,128)S(1)}, f32[64,16,128]{2,1,0:T(8,128)}) custom-call(f32[32,32,128]{2,1,0:T(8,128)S(1)} %all_to_all.31.parts, bf16[4096,256]{1,0:T(8,128)(2,1)S(1)} %get-tuple-element.44.part), custom_call_target="tpu_custom_call" | custom-call | tf_op jit(solution)/shard_map/pallas_call | solution.py:490
  98.6 4.6 %all-to-all-start.4 = ((f32[64,16,128]{2,1,0:T(8,128)}), f32[64,16,128]{2,1,0:T(8,128)S(1)}, u32[]{:S(2)}, u32[]{:S(2)}) async-start(f32[64,16,128]{2,1,0:T(8,128)} %get-tuple-element.48), calls=%async_computation.4 | async-start | bytes 1048576 | tf_op jit(solution)/shard_map/all_to_all | solution.py:571
  103.2 3.4 %collective-permute-start.6 = (f32[32,32]{1,0:T(8,128)S(1)}, f32[32,32]{1,0:T(8,128)S(1)}, u32[]{:S(2)}, u32[]{:S(2)}) collective-permute-start(f32[32,32]{1,0:T(8,128)S(1)} %get-tuple-element.45.a_0_), channel_id=1, source_target_pairs={{0,1},{1,0},{2,3},{3,2},{4,5},{5,4},{6,7},{7,6},{8,9},{9,8},{10,11... | collective-permute-start | bytes 12296 | tf_op jit(solution)/shard_map/ppermute | solution.py:575
  106.7 1.3 collective-permute-start.7
  108.0 0.4 collective-permute-start.8
  108.4 0.0 collective-permute-done.6.a_1_
  108.4 1.3 collective-permute-done.7.a_2_
  109.7 2.9 %collective-permute-done.8.a_3_ = f32[32,32]{1,0:T(8,128)S(1)} collective-permute-done((f32[32,32]{1,0:T(8,128)S(1)}, f32[32,32]{1,0:T(8,128)S(1)}, u32[]{:S(2)}, u32[]{:S(2)}) %collective-permute-start.8) | collective-permute-done | bytes 4128 | tf_op jit(solution)/shard_map/ppermute | solution.py:575
  112.7 1.6 %shard_map.102 = (f32[32,128]{1,0:T(8,128)}, f32[32,32]{1,0:T(8,128)S(1)}) custom-call(f32[32,32]{1,0:T(8,128)S(1)} %get-tuple-element.45.a_0_, f32[32,32]{1,0:T(8,128)S(1)} %collective-permute-done.6.a_1_, f32[32,32]{1,0:T(8,128)S(1)} %collective-permute-done.7.a_2_, f32[32,32]{1,0:T(8,128)S(1)} %collective-permute-done.8.a_3_, ...), custom_call_target="tpu_custom_call" | custom-call | flops 10000000 | bytes 2000000 | tf_op jit(solution)/shard_map/pallas_call | solution.py:510
  114.2 0.0 all-to-all-done.4
  114.2 0.1 reduce_sum.29.own
  114.3 4.5 %collective-permute-start.9 = (f32[16,128]{1,0:T(8,128)S(1)}, f32[16,128]{1,0:T(8,128)S(1)}, u32[]{:S(2)}, u32[]{:S(2)}) collective-permute-start(f32[16,128]{1,0:T(8,128)S(1)} %reduce_sum.29.own), channel_id=1, source_target_pairs={{0,1},{1,0},{2,3},{3,2},{4,5},{5,4},{6,7},{7,6},{8,9},{9,8},{10,11... | collective-permute-start | bytes 24584 | tf_op jit(solution)/shard_map/ppermute | solution.py:567
  118.8 0.8 collective-permute-done.9.other
  119.6 0.4 shard_map.103
  120.0 15.0 %all_to_all.32.own = f32[64,8,128]{2,1,0:T(8,128)S(1)} all-to-all(f32[64,8,128]{2,1,0:T(8,128)S(1)} %shard_map.103), channel_id=1, replica_groups=mesh['y'=4,'h'=2,'z'=4,'l'=2,'c'=2] {'y','h','z','l'}, dimensions={0} | all-to-all | bytes 524288 | tf_op jit(solution)/shard_map/all_to_all | solution.py:571
  135.1 1.6 %collective-permute-start.10 = (f32[64,8,128]{2,1,0:T(8,128)S(1)}, f32[64,8,128]{2,1,0:T(8,128)S(1)}, u32[]{:S(2)}, u32[]{:S(2)}) collective-permute-start(f32[64,8,128]{2,1,0:T(8,128)S(1)} %all_to_all.32.own), channel_id=1, source_target_pairs={{0,1},{1,0},{2,3},{3,2},{4,5},{5,4},{6,7},{7,6},{8,9},{9,8},{10,11... | collective-permute-start | bytes 786440 | tf_op jit(solution)/shard_map/ppermute | solution.py:567
  136.7 1.2 collective-permute-done.10.other
  137.8 0.9 shard_map.104
  (4 shorter events, 0.1 us)
Async XLA Ops:
  0.6 35.2 %copy-start = (f32[2048,64]{0,1:T(8,128)S(1)}, f32[2048,64]{0,1:T(8,128)}, u32[]{:S(2)}) copy-start(f32[2048,64]{0,1:T(8,128)} %param.10) | copy-start | bytes 1572868
  25.6 3.0 %collective-permute-start = (f32[64,128]{1,0:T(8,128)S(1)}, f32[64,128]{1,0:T(8,128)S(1)}, u32[]{:S(2)}, u32[]{:S(2)}) collective-permute-start(f32[64,128]{1,0:T(8,128)S(1)} %reduce_sum.27), channel_id=1, source_target_pairs={{0,1},{1,0},{2,3},{3,2},{4,5},{5,4},{6,7},{7,6},{8,9},{9,8},{10,11... | collective-permute-start | bytes 98312 | tf_op jit(solution)/shard_map/ppermute | solution.py:567
  29.5 13.4 %all-to-all-start.1 = ((f32[8,32,128]{2,1,0:T(8,128)}), f32[8,32,128]{2,1,0:T(8,128)S(1)}, u32[]{:S(2)}, u32[]{:S(2)}) async-start(f32[8,32,128]{2,1,0:T(8,128)} %get-tuple-element.29), calls=%async_computation.1 | async-start | bytes 262144 | tf_op jit(solution)/shard_map/all_to_all | solution.py:571
  46.5 2.6 %collective-permute-start.1 = (f32[32,256]{1,0:T(8,128)S(1)}, f32[32,256]{1,0:T(8,128)S(1)}, u32[]{:S(2)}, u32[]{:S(2)}) collective-permute-start(f32[32,256]{1,0:T(8,128)S(1)} %get-tuple-element.36), channel_id=1, source_target_pairs={{0,1},{1,0},{2,3},{3,2},{4,5},{5,4},{6,7},{7,6},{8,9},{9,8},{10,11... | collective-permute-start | bytes 98312 | tf_op jit(solution)/shard_map/ppermute | solution.py:567
  50.0 15.2 %all-to-all-start.2 = ((f32[16,32,256]{2,1,0:T(8,128)}), f32[16,32,256]{2,1,0:T(8,128)S(1)}, u32[]{:S(2)}, u32[]{:S(2)}) async-start(f32[16,32,256]{2,1,0:T(8,128)} %broadcast_in_dim.12), calls=%async_computation.2 | async-start | bytes 1048576 | tf_op jit(solution)/shard_map/all_to_all | solution.py:571
  53.6 19.4 %copy-start.1 = (f32[4096,32]{0,1:T(8,128)S(1)}, f32[4096,32]{0,1:T(8,128)}, u32[]{:S(2)}) copy-start(f32[4096,32]{0,1:T(8,128)} %param.11) | copy-start | bytes 1572868
  65.2 1.8 %collective-permute-start.2 = (f32[32,256]{1,0:T(8,128)S(1)}, f32[32,256]{1,0:T(8,128)S(1)}, u32[]{:S(2)}, u32[]{:S(2)}) collective-permute-start(f32[32,256]{1,0:T(8,128)S(1)} %reduce_sum.28), channel_id=1, source_target_pairs={{0,1},{1,0},{2,3},{3,2},{4,5},{5,4},{6,7},{7,6},{8,9},{9,8},{10,11... | collective-permute-start | bytes 98312 | tf_op jit(solution)/shard_map/ppermute | solution.py:567
  67.3 3.9 %collective-permute-start.3 = (f32[32,128]{1,0:T(8,128)S(1)}, f32[32,128]{1,0:T(8,128)S(1)}, u32[]{:S(2)}, u32[]{:S(2)}) collective-permute-start(f32[32,128]{1,0:T(8,128)S(1)} %bitcast.18), channel_id=1, source_target_pairs={{0,4},{4,0},{8,12},{12,8},{1,5},{5,1},{9,13},{13,9},{2,6},{6,2},{1... | collective-permute-start | bytes 49160 | tf_op jit(solution)/shard_map/ppermute | solution.py:575
  67.5 4.1 %collective-permute-start.4 = (f32[32,128]{1,0:T(8,128)S(1)}, f32[32,128]{1,0:T(8,128)S(1)}, u32[]{:S(2)}, u32[]{:S(2)}) collective-permute-start(f32[32,128]{1,0:T(8,128)S(1)} %bitcast.19), channel_id=1, source_target_pairs={{0,8},{4,12},{8,0},{12,4},{1,9},{5,13},{9,1},{13,5},{2,10},{6,14},... | collective-permute-start | bytes 49160 | tf_op jit(solution)/shard_map/ppermute | solution.py:575
  69.1 3.9 %collective-permute-start.5 = (f32[32,128]{1,0:T(8,128)S(1)}, f32[32,128]{1,0:T(8,128)S(1)}, u32[]{:S(2)}, u32[]{:S(2)}) collective-permute-start(f32[32,128]{1,0:T(8,128)S(1)} %bitcast.20), channel_id=1, source_target_pairs={{0,12},{4,8},{8,4},{12,0},{1,13},{5,9},{9,5},{13,1},{2,14},{6,10},... | collective-permute-start | bytes 49160 | tf_op jit(solution)/shard_map/ppermute | solution.py:575
  98.6 15.6 %all-to-all-start.4 = ((f32[64,16,128]{2,1,0:T(8,128)}), f32[64,16,128]{2,1,0:T(8,128)S(1)}, u32[]{:S(2)}, u32[]{:S(2)}) async-start(f32[64,16,128]{2,1,0:T(8,128)} %get-tuple-element.48), calls=%async_computation.4 | async-start | bytes 1048576 | tf_op jit(solution)/shard_map/all_to_all | solution.py:571
  103.2 5.2 %collective-permute-start.6 = (f32[32,32]{1,0:T(8,128)S(1)}, f32[32,32]{1,0:T(8,128)S(1)}, u32[]{:S(2)}, u32[]{:S(2)}) collective-permute-start(f32[32,32]{1,0:T(8,128)S(1)} %get-tuple-element.45.a_0_), channel_id=1, source_target_pairs={{0,1},{1,0},{2,3},{3,2},{4,5},{5,4},{6,7},{7,6},{8,9},{9,8},{10,11... | collective-permute-start | bytes 12296 | tf_op jit(solution)/shard_map/ppermute | solution.py:575
  106.7 3.1 %collective-permute-start.7 = (f32[32,32]{1,0:T(8,128)S(1)}, f32[32,32]{1,0:T(8,128)S(1)}, u32[]{:S(2)}, u32[]{:S(2)}) collective-permute-start(f32[32,32]{1,0:T(8,128)S(1)} %get-tuple-element.45.a_0_), channel_id=1, source_target_pairs={{0,2},{1,3},{2,0},{3,1},{4,6},{5,7},{6,4},{7,5},{8,10},{9,11},{10,... | collective-permute-start | bytes 12296 | tf_op jit(solution)/shard_map/ppermute | solution.py:575
  108.0 4.7 %collective-permute-start.8 = (f32[32,32]{1,0:T(8,128)S(1)}, f32[32,32]{1,0:T(8,128)S(1)}, u32[]{:S(2)}, u32[]{:S(2)}) collective-permute-start(f32[32,32]{1,0:T(8,128)S(1)} %get-tuple-element.45.a_0_), channel_id=1, source_target_pairs={{0,3},{1,2},{2,1},{3,0},{4,7},{5,6},{6,5},{7,4},{8,11},{9,10},{10,... | collective-permute-start | bytes 12296 | tf_op jit(solution)/shard_map/ppermute | solution.py:575
  114.3 5.3 %collective-permute-start.9 = (f32[16,128]{1,0:T(8,128)S(1)}, f32[16,128]{1,0:T(8,128)S(1)}, u32[]{:S(2)}, u32[]{:S(2)}) collective-permute-start(f32[16,128]{1,0:T(8,128)S(1)} %reduce_sum.29.own), channel_id=1, source_target_pairs={{0,1},{1,0},{2,3},{3,2},{4,5},{5,4},{6,7},{7,6},{8,9},{9,8},{10,11... | collective-permute-start | bytes 24584 | tf_op jit(solution)/shard_map/ppermute | solution.py:567
  135.1 2.8 %collective-permute-start.10 = (f32[64,8,128]{2,1,0:T(8,128)S(1)}, f32[64,8,128]{2,1,0:T(8,128)S(1)}, u32[]{:S(2)}, u32[]{:S(2)}) collective-permute-start(f32[64,8,128]{2,1,0:T(8,128)S(1)} %all_to_all.32.own), channel_id=1, source_target_pairs={{0,1},{1,0},{2,3},{3,2},{4,5},{5,4},{6,7},{7,6},{8,9},{9,8},{10,11... | collective-permute-start | bytes 786440 | tf_op jit(solution)/shard_map/ppermute | solution.py:567

commit v4 on v3

--- a/solution.py
+++ b/solution.py
@@ -326,18 +326,22 @@
     )(core_id, grams, z, sk, u)
 
 
+def chunk_sizes(n):
+    return [16] + [32] * ((n - 32) // 32) + [16]
+
+
 def contract_x_kernel(q, field, wx, held, out, lhs, sems, out_sems):
     nx, ny, nt = held.shape
     r1 = q.shape[0]
-    chunks = sems.shape[0]
-    rows = ny // chunks
+    sizes = chunk_sizes(ny)
+    chunks = len(sizes)
 
     def copy(i):
-        s = pl.ds(pl.multiple_of(i * rows, 8), rows)
+        s = pl.ds(sum(sizes[:i]), sizes[i])
         return pltpu.make_async_copy(field.at[:, s, :], held.at[:, s, :], sems.at[i])
 
     def copy_out(i):
-        s = pl.ds(pl.multiple_of(i * rows, 8), rows)
+        s = pl.ds(sum(sizes[:i]), sizes[i])
         return pltpu.make_async_copy(
             out.at[:, s, :], wx.at[pl.ds(0, r1), s, :], out_sems.at[i]
         )
@@ -346,15 +350,12 @@
         copy(i).start()
     lhs[...] = twice(q[...])
 
-    def chunk(i, _):
+    for i in range(chunks):
         copy(i).wait()
-
-        @pl.when(i + AHEAD < chunks)
-        def _():
+        if i + AHEAD < chunks:
             copy(i + AHEAD).start()
-
-        for y8 in range(0, rows, 8):
-            at = pl.multiple_of(i * rows + y8, 8)
+        for y8 in range(0, sizes[i], 8):
+            at = sum(sizes[:i]) + y8
             f = jnp.swapaxes(held[:, pl.ds(at, 8), :], 0, 1)
             outs = []
             for y in range(0, 8, 2):
@@ -368,9 +369,6 @@
                 outs += [o[:, :nt], o[:, nt:]]
             out[:, pl.ds(at, 8), :] = jnp.swapaxes(jnp.stack(outs, 0), 0, 1)
         copy_out(i).start()
-        return 0
-
-    lax.fori_loop(0, chunks, chunk, 0)
     for i in range(chunks):
         copy_out(i).wait()
 
@@ -378,7 +376,7 @@
 def contract_x(q, field):
     nx, ny, nt = field.shape
     r1 = q.shape[0]
-    chunks = ny // 32
+    chunks = len(chunk_sizes(ny))
     return pl.pallas_call(
         contract_x_kernel,
         in_specs=[VMEM, HBM],

time: 139 us -> 139 us (level)
  no operation moved by 1% of the time
where the time goes in v4:
time: 139 us; the launch traced here: 138 us
  blocking collectives  46.4 us (33%)
  Pallas kernels  41.3 us (30%)
  starting transfers between devices  35 us (25%)
  waiting for transfers between devices  13.9 us (10%)
    all_to_all x3, blocking collectives, exchange(): return lax.all_to_all(x, axes, 0, 0)  46.4 us
    all_to_all x3, starting transfers between devices, exchange(): return lax.all_to_all(x, axes, 0, 0)  14.7 us
    pallas_call x1, Pallas kernels, first(): pl.pallas_call(first_kernel, in_specs=[HBM, HBM, HBM, HBM], out_specs=[HB...  11.9 us
    ppermute x5, starting transfers between devices, pair(): return lax.ppermute(x, 'c', [(0, 1), (1, 0)])  11.2 us
    pallas_call x1, Pallas kernels, contract_x(): pl.pallas_call(contract_x_kernel, in_specs=[VMEM, HBM], out_specs=HBM, ou...  11.2 us
    ppermute x6, starting transfers between devices, of_four(): lax.ppermute(x, axes, [(i, i ^ s) for i in range(4)])  9.05 us
    ppermute x6, waiting for transfers between devices, of_four(): lax.ppermute(x, axes, [(i, i ^ s) for i in range(4)])  6.1 us
    pallas_call x1, Pallas kernels, third(): pl.pallas_call(lambda *a: third_kernel(scale, *a), in_specs=[VMEM] * 6 +...  5.06 us
  transfers between devices with their start and end apart: 14, of which 10 were waited for; matrix products, arithmetic and copies ran while one was open for 0% of the time, Pallas kernels for 12%

profile of v4, /device:TPU:1, one launch (start us, length us, event | category | flops | bytes accessed | tf_op | source)
XLA Modules:
  0.0 138.4 jit_solution(18431949962544212085)
XLA Ops:
  0.6 0.0 copy-start
  0.6 11.9 %shard_map.93 = (bf16[128,256,256]{2,1,0:T(8,128)(2,1)}, f32[8,64,128]{2,1,0:T(8,128)}) custom-call(f32[128,256,128]{2,1,0:T(8,128)} %field.3, f32[32,128]{1,0:T(8,128)} %bitcast.26, f32[64,256]{1,0:T(8,128)} %bitcast.24, f32[64,2048]{1,0:T(8,128)} %bitcast.22), custom_call_target="tpu_custom_call" | custom-call | flops 1073741824 | bytes 16777216 | tf_op jit(solution)/shard_map/pallas_call | solution.py:174
  12.6 13.0 %all_to_all.30 = f32[8,64,128]{2,1,0:T(8,128)S(1)} all-to-all(f32[8,64,128]{2,1,0:T(8,128)} %get-tuple-element.28), channel_id=1, replica_groups=mesh['y'=4,'h'=2,'z'=4,'l'=2,'c'=2] {'z','l'}, dimensions={0} | all-to-all | bytes 524288 | tf_op jit(solution)/shard_map/all_to_all | solution.py:569
  25.6 2.1 %collective-permute-start = (f32[64,128]{1,0:T(8,128)S(1)}, f32[64,128]{1,0:T(8,128)S(1)}, u32[]{:S(2)}, u32[]{:S(2)}) collective-permute-start(f32[64,128]{1,0:T(8,128)S(1)} %reduce_sum.27), channel_id=1, source_target_pairs={{0,1},{1,0},{2,3},{3,2},{4,5},{5,4},{6,7},{7,6},{8,9},{9,8},{10,11... | collective-permute-start | bytes 98312 | tf_op jit(solution)/shard_map/ppermute | solution.py:565
  27.7 0.9 collective-permute-done
  28.6 0.9 shard_map.94
  29.5 6.4 %all-to-all-start.1 = ((f32[8,32,128]{2,1,0:T(8,128)}), f32[8,32,128]{2,1,0:T(8,128)S(1)}, u32[]{:S(2)}, u32[]{:S(2)}) async-start(f32[8,32,128]{2,1,0:T(8,128)} %get-tuple-element.29), calls=%async_computation.1 | async-start | bytes 262144 | tf_op jit(solution)/shard_map/all_to_all | solution.py:569
  35.9 0.0 copy-done
  35.9 1.1 shard_map.96.a_3_
  37.0 2.7 %shard_map.95.a_4_ = bf16[2048,512]{1,0:T(8,128)(2,1)S(1)} custom-call(f32[64,128]{1,0:T(8,128)S(1)} %get-tuple-element.30.z.a_2_, bf16[128,256,256]{2,1,0:T(8,128)(2,1)} %get-tuple-element.31.w), custom_call_target="tpu_custom_call" | custom-call | flops 1000000000 | bytes 6000000 | tf_op jit(solution)/shard_map/pallas_call | solution.py:273
  39.7 3.2 %all-to-all-done.1.a_1_ = f32[8,32,128]{2,1,0:T(8,128)S(1)} async-done(((f32[8,32,128]{2,1,0:T(8,128)}), f32[8,32,128]{2,1,0:T(8,128)S(1)}, u32[]{:S(2)}, u32[]{:S(2)}) %all-to-all-start.1) | async-done | bytes 131104 | tf_op jit(solution)/shard_map/all_to_all | solution.py:569
  42.9 3.6 %shard_map.97 = (f32[64,128]{1,0:T(8,128)S(1)}, f32[64,128]{1,0:T(8,128)}, f32[32,256]{1,0:T(8,128)S(1)}, f32[32,256]{1,0:T(8,128)S(1)}) custom-call(s32[1]{0:T(128)} %bitcast.a_0_.core_id, f32[8,32,128]{2,1,0:T(8,128)S(1)} %all-to-all-done.1.a_1_, f32[64,128]{1,0:T(8,128)S(1)} %get-tuple-element.30.z.a_2_, bf16[2048,256]{1,0:T(8,128)(2,1)S(1)} %shard_map.96.a_3_, ...), custom_call_target="tpu_custom_call" | custom-call | tf_op jit(solution)/shard_map/pallas_call | solution.py:315
  46.5 1.8 %collective-permute-start.1 = (f32[32,256]{1,0:T(8,128)S(1)}, f32[32,256]{1,0:T(8,128)S(1)}, u32[]{:S(2)}, u32[]{:S(2)}) collective-permute-start(f32[32,256]{1,0:T(8,128)S(1)} %get-tuple-element.36), channel_id=1, source_target_pairs={{0,1},{1,0},{2,3},{3,2},{4,5},{5,4},{6,7},{7,6},{8,9},{9,8},{10,11... | collective-permute-start | bytes 98312 | tf_op jit(solution)/shard_map/ppermute | solution.py:565
  48.3 0.9 collective-permute-done.1
  49.2 0.8 broadcast_in_dim.12
  50.0 3.8 %all-to-all-start.2 = ((f32[16,32,256]{2,1,0:T(8,128)}), f32[16,32,256]{2,1,0:T(8,128)S(1)}, u32[]{:S(2)}, u32[]{:S(2)}) async-start(f32[16,32,256]{2,1,0:T(8,128)} %broadcast_in_dim.12), calls=%async_computation.2 | async-start | bytes 1048576 | tf_op jit(solution)/shard_map/all_to_all | solution.py:569
  53.8 0.0 copy-start.1
  53.8 11.2 %shard_map.98.a_6_ = f32[128,256,128]{2,1,0:T(8,128)} custom-call(f32[64,128]{1,0:T(8,128)S(1)} %get-tuple-element.37.q, f32[128,256,128]{2,1,0:T(8,128)} %field.3), custom_call_target="tpu_custom_call" | custom-call | flops 2147483648 | bytes 25165824 | tf_op jit(solution)/shard_map/pallas_call | solution.py:380
  65.0 0.0 all-to-all-done.2
  65.0 1.1 collective-permute-start.2
  66.2 0.9 collective-permute-done.2
  67.0 0.3 shard_map.99
  67.3 0.3 collective-permute-start.3
  67.5 1.6 %collective-permute-start.4 = (f32[32,128]{1,0:T(8,128)S(1)}, f32[32,128]{1,0:T(8,128)S(1)}, u32[]{:S(2)}, u32[]{:S(2)}) collective-permute-start(f32[32,128]{1,0:T(8,128)S(1)} %bitcast.19), channel_id=1, source_target_pairs={{0,8},{4,12},{8,0},{12,4},{1,9},{5,13},{9,1},{13,5},{2,10},{6,14},... | collective-permute-start | bytes 49160 | tf_op jit(solution)/shard_map/ppermute | solution.py:573
  69.1 2.0 %collective-permute-start.5 = (f32[32,128]{1,0:T(8,128)S(1)}, f32[32,128]{1,0:T(8,128)S(1)}, u32[]{:S(2)}, u32[]{:S(2)}) collective-permute-start(f32[32,128]{1,0:T(8,128)S(1)} %bitcast.20), channel_id=1, source_target_pairs={{0,12},{4,8},{8,4},{12,0},{1,13},{5,9},{9,5},{13,1},{2,14},{6,10},... | collective-permute-start | bytes 49160 | tf_op jit(solution)/shard_map/ppermute | solution.py:573
  71.2 0.0 collective-permute-done.3.a_1_
  71.2 0.4 collective-permute-done.4.a_2_
  71.6 1.4 %collective-permute-done.5.a_3_ = f32[32,128]{1,0:T(8,128)S(1)} collective-permute-done((f32[32,128]{1,0:T(8,128)S(1)}, f32[32,128]{1,0:T(8,128)S(1)}, u32[]{:S(2)}, u32[]{:S(2)}) %collective-permute-start.5) | collective-permute-done | bytes 16416 | tf_op jit(solution)/shard_map/ppermute | solution.py:573
  73.0 0.0 copy-done.1
  73.0 5.1 %shard_map.100 = (f32[64,256]{1,0:T(8,128)}, bf16[4096,256]{1,0:T(8,128)(2,1)S(1)}, f32[32,32,128]{2,1,0:T(8,128)S(1)}) custom-call(f32[32,128]{1,0:T(8,128)S(1)} %bitcast.21, f32[32,128]{1,0:T(8,128)S(1)} %collective-permute-done.3.a_1_, f32[32,128]{1,0:T(8,128)S(1)} %collective-permute-done.4.a_2_, f32[32,128]{1,0:T(8,128)S(1)} %collective-permute-done.5.a_3_, ...), custom_call_target="tpu_custom_call" | custom-call | tf_op jit(solution)/shard_map/pallas_call | solution.py:450
  78.1 18.4 %all_to_all.31.parts = f32[32,32,128]{2,1,0:T(8,128)S(1)} all-to-all(f32[32,32,128]{2,1,0:T(8,128)S(1)} %get-tuple-element.43), channel_id=1, replica_groups=mesh['y'=4,'h'=2,'z'=4,'l'=2,'c'=2] {'y','h','z'}, dimensions={0} | all-to-all | bytes 1048576 | tf_op jit(solution)/shard_map/all_to_all | solution.py:569
  96.5 1.7 %shard_map.101 = (f32[32,128]{1,0:T(8,128)S(1)}, f32[32,32]{1,0:T(8,128)S(1)}, f32[64,16,128]{2,1,0:T(8,128)}) custom-call(f32[32,32,128]{2,1,0:T(8,128)S(1)} %all_to_all.31.parts, bf16[4096,256]{1,0:T(8,128)(2,1)S(1)} %get-tuple-element.44.part), custom_call_target="tpu_custom_call" | custom-call | tf_op jit(solution)/shard_map/pallas_call | solution.py:488
  98.2 4.6 %all-to-all-start.4 = ((f32[64,16,128]{2,1,0:T(8,128)}), f32[64,16,128]{2,1,0:T(8,128)S(1)}, u32[]{:S(2)}, u32[]{:S(2)}) async-start(f32[64,16,128]{2,1,0:T(8,128)} %get-tuple-element.48), calls=%async_computation.4 | async-start | bytes 1048576 | tf_op jit(solution)/shard_map/all_to_all | solution.py:569
  102.9 3.4 %collective-permute-start.6 = (f32[32,32]{1,0:T(8,128)S(1)}, f32[32,32]{1,0:T(8,128)S(1)}, u32[]{:S(2)}, u32[]{:S(2)}) collective-permute-start(f32[32,32]{1,0:T(8,128)S(1)} %get-tuple-element.45.a_0_), channel_id=1, source_target_pairs={{0,1},{1,0},{2,3},{3,2},{4,5},{5,4},{6,7},{7,6},{8,9},{9,8},{10,11... | collective-permute-start | bytes 12296 | tf_op jit(solution)/shard_map/ppermute | solution.py:573
  106.3 1.3 collective-permute-start.7
  107.6 0.4 collective-permute-start.8
  108.0 0.0 collective-permute-done.6.a_1_
  108.0 1.3 collective-permute-done.7.a_2_
  109.4 2.9 %collective-permute-done.8.a_3_ = f32[32,32]{1,0:T(8,128)S(1)} collective-permute-done((f32[32,32]{1,0:T(8,128)S(1)}, f32[32,32]{1,0:T(8,128)S(1)}, u32[]{:S(2)}, u32[]{:S(2)}) %collective-permute-start.8) | collective-permute-done | bytes 4128 | tf_op jit(solution)/shard_map/ppermute | solution.py:573
  112.3 1.6 %shard_map.102 = (f32[32,128]{1,0:T(8,128)}, f32[32,32]{1,0:T(8,128)S(1)}) custom-call(f32[32,32]{1,0:T(8,128)S(1)} %get-tuple-element.45.a_0_, f32[32,32]{1,0:T(8,128)S(1)} %collective-permute-done.6.a_1_, f32[32,32]{1,0:T(8,128)S(1)} %collective-permute-done.7.a_2_, f32[32,32]{1,0:T(8,128)S(1)} %collective-permute-done.8.a_3_, ...), custom_call_target="tpu_custom_call" | custom-call | flops 10000000 | bytes 2000000 | tf_op jit(solution)/shard_map/pallas_call | solution.py:508
  113.8 0.0 all-to-all-done.4
  113.9 0.1 reduce_sum.29.own
  113.9 4.5 %collective-permute-start.9 = (f32[16,128]{1,0:T(8,128)S(1)}, f32[16,128]{1,0:T(8,128)S(1)}, u32[]{:S(2)}, u32[]{:S(2)}) collective-permute-start(f32[16,128]{1,0:T(8,128)S(1)} %reduce_sum.29.own), channel_id=1, source_target_pairs={{0,1},{1,0},{2,3},{3,2},{4,5},{5,4},{6,7},{7,6},{8,9},{9,8},{10,11... | collective-permute-start | bytes 24584 | tf_op jit(solution)/shard_map/ppermute | solution.py:565
  118.4 0.8 collective-permute-done.9.other
  119.3 0.4 shard_map.103
  119.6 15.0 %all_to_all.32.own = f32[64,8,128]{2,1,0:T(8,128)S(1)} all-to-all(f32[64,8,128]{2,1,0:T(8,128)S(1)} %shard_map.103), channel_id=1, replica_groups=mesh['y'=4,'h'=2,'z'=4,'l'=2,'c'=2] {'y','h','z','l'}, dimensions={0} | all-to-all | bytes 524288 | tf_op jit(solution)/shard_map/all_to_all | solution.py:569
  134.7 1.6 %collective-permute-start.10 = (f32[64,8,128]{2,1,0:T(8,128)S(1)}, f32[64,8,128]{2,1,0:T(8,128)S(1)}, u32[]{:S(2)}, u32[]{:S(2)}) collective-permute-start(f32[64,8,128]{2,1,0:T(8,128)S(1)} %all_to_all.32.own), channel_id=1, source_target_pairs={{0,1},{1,0},{2,3},{3,2},{4,5},{5,4},{6,7},{7,6},{8,9},{9,8},{10,11... | collective-permute-start | bytes 786440 | tf_op jit(solution)/shard_map/ppermute | solution.py:565
  136.3 1.2 collective-permute-done.10.other
  137.5 0.9 shard_map.104
  (4 shorter events, 0.1 us)
Async XLA Ops:
  0.6 35.2 %copy-start = (f32[2048,64]{0,1:T(8,128)S(1)}, f32[2048,64]{0,1:T(8,128)}, u32[]{:S(2)}) copy-start(f32[2048,64]{0,1:T(8,128)} %param.10) | copy-start | bytes 1572868
  25.6 3.0 %collective-permute-start = (f32[64,128]{1,0:T(8,128)S(1)}, f32[64,128]{1,0:T(8,128)S(1)}, u32[]{:S(2)}, u32[]{:S(2)}) collective-permute-start(f32[64,128]{1,0:T(8,128)S(1)} %reduce_sum.27), channel_id=1, source_target_pairs={{0,1},{1,0},{2,3},{3,2},{4,5},{5,4},{6,7},{7,6},{8,9},{9,8},{10,11... | collective-permute-start | bytes 98312 | tf_op jit(solution)/shard_map/ppermute | solution.py:565
  29.5 13.4 %all-to-all-start.1 = ((f32[8,32,128]{2,1,0:T(8,128)}), f32[8,32,128]{2,1,0:T(8,128)S(1)}, u32[]{:S(2)}, u32[]{:S(2)}) async-start(f32[8,32,128]{2,1,0:T(8,128)} %get-tuple-element.29), calls=%async_computation.1 | async-start | bytes 262144 | tf_op jit(solution)/shard_map/all_to_all | solution.py:569
  46.5 2.6 %collective-permute-start.1 = (f32[32,256]{1,0:T(8,128)S(1)}, f32[32,256]{1,0:T(8,128)S(1)}, u32[]{:S(2)}, u32[]{:S(2)}) collective-permute-start(f32[32,256]{1,0:T(8,128)S(1)} %get-tuple-element.36), channel_id=1, source_target_pairs={{0,1},{1,0},{2,3},{3,2},{4,5},{5,4},{6,7},{7,6},{8,9},{9,8},{10,11... | collective-permute-start | bytes 98312 | tf_op jit(solution)/shard_map/ppermute | solution.py:565
  50.0 15.0 %all-to-all-start.2 = ((f32[16,32,256]{2,1,0:T(8,128)}), f32[16,32,256]{2,1,0:T(8,128)S(1)}, u32[]{:S(2)}, u32[]{:S(2)}) async-start(f32[16,32,256]{2,1,0:T(8,128)} %broadcast_in_dim.12), calls=%async_computation.2 | async-start | bytes 1048576 | tf_op jit(solution)/shard_map/all_to_all | solution.py:569
  53.8 19.2 %copy-start.1 = (f32[4096,32]{0,1:T(8,128)S(1)}, f32[4096,32]{0,1:T(8,128)}, u32[]{:S(2)}) copy-start(f32[4096,32]{0,1:T(8,128)} %param.11) | copy-start | bytes 1572868
  65.0 2.0 %collective-permute-start.2 = (f32[32,256]{1,0:T(8,128)S(1)}, f32[32,256]{1,0:T(8,128)S(1)}, u32[]{:S(2)}, u32[]{:S(2)}) collective-permute-start(f32[32,256]{1,0:T(8,128)S(1)} %reduce_sum.28), channel_id=1, source_target_pairs={{0,1},{1,0},{2,3},{3,2},{4,5},{5,4},{6,7},{7,6},{8,9},{9,8},{10,11... | collective-permute-start | bytes 98312 | tf_op jit(solution)/shard_map/ppermute | solution.py:565
  67.3 3.9 %collective-permute-start.3 = (f32[32,128]{1,0:T(8,128)S(1)}, f32[32,128]{1,0:T(8,128)S(1)}, u32[]{:S(2)}, u32[]{:S(2)}) collective-permute-start(f32[32,128]{1,0:T(8,128)S(1)} %bitcast.18), channel_id=1, source_target_pairs={{0,4},{4,0},{8,12},{12,8},{1,5},{5,1},{9,13},{13,9},{2,6},{6,2},{1... | collective-permute-start | bytes 49160 | tf_op jit(solution)/shard_map/ppermute | solution.py:573
  67.5 4.1 %collective-permute-start.4 = (f32[32,128]{1,0:T(8,128)S(1)}, f32[32,128]{1,0:T(8,128)S(1)}, u32[]{:S(2)}, u32[]{:S(2)}) collective-permute-start(f32[32,128]{1,0:T(8,128)S(1)} %bitcast.19), channel_id=1, source_target_pairs={{0,8},{4,12},{8,0},{12,4},{1,9},{5,13},{9,1},{13,5},{2,10},{6,14},... | collective-permute-start | bytes 49160 | tf_op jit(solution)/shard_map/ppermute | solution.py:573
  69.1 3.9 %collective-permute-start.5 = (f32[32,128]{1,0:T(8,128)S(1)}, f32[32,128]{1,0:T(8,128)S(1)}, u32[]{:S(2)}, u32[]{:S(2)}) collective-permute-start(f32[32,128]{1,0:T(8,128)S(1)} %bitcast.20), channel_id=1, source_target_pairs={{0,12},{4,8},{8,4},{12,0},{1,13},{5,9},{9,5},{13,1},{2,14},{6,10},... | collective-permute-start | bytes 49160 | tf_op jit(solution)/shard_map/ppermute | solution.py:573
  98.2 15.6 %all-to-all-start.4 = ((f32[64,16,128]{2,1,0:T(8,128)}), f32[64,16,128]{2,1,0:T(8,128)S(1)}, u32[]{:S(2)}, u32[]{:S(2)}) async-start(f32[64,16,128]{2,1,0:T(8,128)} %get-tuple-element.48), calls=%async_computation.4 | async-start | bytes 1048576 | tf_op jit(solution)/shard_map/all_to_all | solution.py:569
  102.9 5.2 %collective-permute-start.6 = (f32[32,32]{1,0:T(8,128)S(1)}, f32[32,32]{1,0:T(8,128)S(1)}, u32[]{:S(2)}, u32[]{:S(2)}) collective-permute-start(f32[32,32]{1,0:T(8,128)S(1)} %get-tuple-element.45.a_0_), channel_id=1, source_target_pairs={{0,1},{1,0},{2,3},{3,2},{4,5},{5,4},{6,7},{7,6},{8,9},{9,8},{10,11... | collective-permute-start | bytes 12296 | tf_op jit(solution)/shard_map/ppermute | solution.py:573
  106.3 3.1 %collective-permute-start.7 = (f32[32,32]{1,0:T(8,128)S(1)}, f32[32,32]{1,0:T(8,128)S(1)}, u32[]{:S(2)}, u32[]{:S(2)}) collective-permute-start(f32[32,32]{1,0:T(8,128)S(1)} %get-tuple-element.45.a_0_), channel_id=1, source_target_pairs={{0,2},{1,3},{2,0},{3,1},{4,6},{5,7},{6,4},{7,5},{8,10},{9,11},{10,... | collective-permute-start | bytes 12296 | tf_op jit(solution)/shard_map/ppermute | solution.py:573
  107.6 4.7 %collective-permute-start.8 = (f32[32,32]{1,0:T(8,128)S(1)}, f32[32,32]{1,0:T(8,128)S(1)}, u32[]{:S(2)}, u32[]{:S(2)}) collective-permute-start(f32[32,32]{1,0:T(8,128)S(1)} %get-tuple-element.45.a_0_), channel_id=1, source_target_pairs={{0,3},{1,2},{2,1},{3,0},{4,7},{5,6},{6,5},{7,4},{8,11},{9,10},{10,... | collective-permute-start | bytes 12296 | tf_op jit(solution)/shard_map/ppermute | solution.py:573
  113.9 5.3 %collective-permute-start.9 = (f32[16,128]{1,0:T(8,128)S(1)}, f32[16,128]{1,0:T(8,128)S(1)}, u32[]{:S(2)}, u32[]{:S(2)}) collective-permute-start(f32[16,128]{1,0:T(8,128)S(1)} %reduce_sum.29.own), channel_id=1, source_target_pairs={{0,1},{1,0},{2,3},{3,2},{4,5},{5,4},{6,7},{7,6},{8,9},{9,8},{10,11... | collective-permute-start | bytes 24584 | tf_op jit(solution)/shard_map/ppermute | solution.py:565
  134.7 2.8 %collective-permute-start.10 = (f32[64,8,128]{2,1,0:T(8,128)S(1)}, f32[64,8,128]{2,1,0:T(8,128)S(1)}, u32[]{:S(2)}, u32[]{:S(2)}) collective-permute-start(f32[64,8,128]{2,1,0:T(8,128)S(1)} %all_to_all.32.own), channel_id=1, source_target_pairs={{0,1},{1,0},{2,3},{3,2},{4,5},{5,4},{6,7},{7,6},{8,9},{9,8},{10,11... | collective-permute-start | bytes 786440 | tf_op jit(solution)/shard_map/ppermute | solution.py:565
